TPU v7x, 512 devices: a whole 4x4x16 slice. The times are simulated.
512 devices in a mesh: tm: 128 (over y_hi, z, x), height: 4 (over y_lo, core).
Axes of the slice: x: 4, y: 4 (y_hi: 2, y_lo: 2; y = y_hi * 2 + y_lo), z: 16, core: 2. Of those that a mesh axis runs over, the one named last changes fastest.
Arguments:
- frames_in: bfloat16 [512, 320, 512], P('tm', None, 'height'), may hold values from -6 to 6
- conv_spatial: bfloat16 [320, 2880], replicated, may hold values from -0.109375 to 0.109375
- conv_temporal: bfloat16 [320, 960], replicated, may hold values from -0.1875 to 0.1875
- w_query: bfloat16 [320, 320], replicated, may hold values from -2 to 2
- w_key: bfloat16 [320, 320], replicated, may hold values from -2 to 2
- w_value: bfloat16 [320, 320], replicated, may hold values from -0.3125 to 0.3125
- w_out: bfloat16 [320, 320], replicated, may hold values from -0.3125 to 0.3125
- win_left: int32 [5], replicated, may hold values from 0 to 8, as said below
- win_right: int32 [5], replicated, may hold values from 0 to 8, as said below
Outputs:
- frames_out: bfloat16 [512, 320, 512], P('tm', None, 'height')
Inputs may be any that keep to these rules, and one draw needn't show every extreme that they name: `win_left`: some head reaches back exactly 8 frames. `win_right`: some head reaches ahead exactly 8 frames.
All inputs are finite; a program needn't handle non-finite values.
Results may differ from a plain program's by a relative error of at most 0.017.
Values may be sent and summed in bfloat16 or wider, within the bound.
A program may use at most 64 MiB of HBM per device.

v0:
```python
import jax
import jax.numpy as jnp
from jax import lax
from jax.sharding import PartitionSpec as P

HEADS = 5
HEAD_DIM = 64
WIDE = 32
WMAX = 8


def padded_2(cells, sides, width):
    for axis, dim in sides:
        count = lax.axis_size(axis)
        ends = count - 1
        head = lax.slice_in_dim(cells, 0, width, axis=dim)
        tail = lax.slice_in_dim(cells, cells.shape[dim] - width, cells.shape[dim], axis=dim)
        cells = jnp.concatenate(
            [
                lax.ppermute(tail, axis, [(i, (i + 1) % count) for i in range(ends)]),
                cells,
                lax.ppermute(head, axis, [((i + 1) % count, i) for i in range(ends)]),
            ],
            axis=dim,
        )
    return cells


def shifted(value, axis, steps):
    count = lax.axis_size(axis)
    leading, last = (max(0, -steps), min(count, count - steps))
    return lax.ppermute(value, axis, [(source, source + steps) for source in range(leading, last)])


def silu_round(source):
    widened = source.astype(jnp.float32)
    return jax.nn.silu(widened).astype(jnp.bfloat16)


def layer_norm(stream):
    widened = stream.astype(jnp.float32)
    centred = widened - jnp.mean(widened, axis=1, keepdims=True)
    spread = jnp.mean(centred * centred, axis=1, keepdims=True)
    return (centred * lax.rsqrt(spread + 1e-05)).astype(jnp.bfloat16)


def project(weight, source):
    return jnp.einsum("oi,fip->fop", weight, source, preferred_element_type=jnp.float32).astype(
        jnp.bfloat16
    )


def attend(
    queries, key_frames, value_frames, first_query, first_key, win_left, win_right, total_frames
):
    query_count = queries.shape[0]
    key_count = key_frames.shape[0]
    cell_count = queries.shape[2]
    query_heads = queries.reshape(query_count, HEADS, HEAD_DIM, cell_count)
    key_heads = key_frames.reshape(key_count, HEADS, HEAD_DIM, cell_count)
    value_heads = value_frames.reshape(key_count, HEADS, HEAD_DIM, cell_count)
    scores = jnp.einsum(
        "thdp,shdp->tshp", query_heads, key_heads, preferred_element_type=jnp.float32
    ) * HEAD_DIM ** (-0.5)
    query_pos = first_query + jnp.arange(query_count, dtype=jnp.int32)
    key_pos = first_key + jnp.arange(key_count, dtype=jnp.int32)
    offset = key_pos[None, :, None] - query_pos[:, None, None]
    inside = (key_pos >= 0) & (key_pos < total_frames)
    allowed = (
        (offset >= -win_left[None, None, :])
        & (offset <= win_right[None, None, :])
        & inside[None, :, None]
    )
    masked = jnp.where(allowed[..., None], scores, -1e30)
    highest = jnp.max(masked, axis=1, keepdims=True)
    raised = jnp.exp(masked - highest)
    weights = (raised / jnp.sum(raised, axis=1, keepdims=True)).astype(jnp.bfloat16)
    blended = jnp.einsum(
        "tshp,shdp->thdp", weights, value_heads, preferred_element_type=jnp.float32
    )
    return blended.reshape(query_count, HEADS * HEAD_DIM, cell_count).astype(jnp.bfloat16)


def per_device(
    frames_in, conv_spatial, conv_temporal, w_query, w_key, w_value, w_out, win_left, win_right
):
    frame_count, channels, cell_count = frames_in.shape
    row_count = cell_count // WIDE
    active = silu_round(frames_in)
    lattice = active.reshape(frame_count, channels, row_count, WIDE)
    rimmed = padded_2(lattice, (("height", 2),), 1)
    padded = jnp.pad(rimmed, ((0, 0), (0, 0), (0, 0), (1, 1)))
    tap_list = [
        padded[:, :, row_step : row_step + row_count, col_step : col_step + WIDE]
        for row_step in range(3)
        for col_step in range(3)
    ]
    stacked = jnp.concatenate(tap_list, axis=1)
    spatial = jnp.einsum("oj,fjrw->forw", conv_spatial, stacked, preferred_element_type=jnp.float32)
    settled = (
        frames_in.astype(jnp.float32) + spatial.reshape(frame_count, channels, cell_count)
    ).astype(jnp.bfloat16)
    moving = silu_round(settled)
    framed = padded_2(moving, (("tm", 0),), 1)
    stacked_time = jnp.concatenate(
        [framed[0:frame_count], framed[1 : frame_count + 1], framed[2 : frame_count + 2]], axis=1
    )
    temporal = jnp.einsum(
        "oj,fjp->fop", conv_temporal, stacked_time, preferred_element_type=jnp.float32
    )
    stream = (settled.astype(jnp.float32) + temporal).astype(jnp.bfloat16)
    normed = layer_norm(stream)
    queries = project(w_query, normed)
    reach_count = WMAX // frame_count
    paired = jnp.stack([project(w_key, normed), project(w_value, normed)], axis=1)
    before_list = [shifted(paired, "tm", distance) for distance in range(reach_count, 0, -1)]
    after_list = [shifted(paired, "tm", -distance) for distance in range(1, reach_count + 1)]
    joined = jnp.concatenate(before_list + [paired] + after_list, axis=0)
    key_frames = joined[:, 0]
    value_frames = joined[:, 1]
    first_query = lax.axis_index("tm") * frame_count
    total_frames = frame_count * lax.axis_size("tm")
    blended = attend(
        queries,
        key_frames,
        value_frames,
        first_query,
        first_query - WMAX,
        win_left,
        win_right,
        total_frames,
    )
    mixed_out = jnp.einsum("oi,fip->fop", w_out, blended, preferred_element_type=jnp.float32)
    return (stream.astype(jnp.float32) + mixed_out).astype(jnp.bfloat16)


def solution(mesh):
    return jax.shard_map(
        per_device,
        mesh=mesh,
        in_specs=(P("tm", None, "height"), P(), P(), P(), P(), P(), P(), P(), P()),
        out_specs=P("tm", None, "height"),
        check_vma=False,
    )
```

profile of v0, /device:TPU:97, one launch (start us, length us, event | category | flops | bytes accessed | tf_op | source)
XLA Modules:
  0.0 128.8 jit_solution(16228343463170449611)
XLA Ops:
  0.0 0.0 copy-start
  0.0 1.3 %fusion.31 = bf16[4,320,128]{2,1,0:T(8,128)(2,1)S(1)} fusion(bf16[4,320,128]{2,1,0:T(8,128)(2,1)} %param.9), kind=kLoop, calls=%fused_computation.46 | loop fusion | flops 983040 | bytes 655360 | tf_op jit(solution)/shard_map/convert_element_type | solution.py:37
  1.3 0.2 copy.15
  1.6 3.8 %collective-permute-start = (bf16[4,320,1,32]{1,3,2,0:T(8,128)(2,1)S(1)}, bf16[4,320,1,32]{1,3,2,0:T(8,128)(2,1)S(1)}, u32[]{:S(2)}, u32[]{:S(2)}) collective-permute-start(bf16[4,320,1,32]{1,3,2,0:T(8,128)(2,1)S(1)} %get-tuple-element.15), channel_id=1, source_target_pairs={{0,1},{1,2},{2,3},{4,5},{5,6},{6,7},{8,9},{9,10},{10,11},{12,13},{... | collective-permute-start | bytes 245768 | tf_op jit(solution)/shard_map/ppermute | solution.py:20
  5.3 1.9 %collective-permute-start.1 = (bf16[4,320,1,32]{1,3,2,0:T(8,128)(2,1)S(1)}, bf16[4,320,1,32]{1,3,2,0:T(8,128)(2,1)S(1)}, u32[]{:S(2)}, u32[]{:S(2)}) collective-permute-start(bf16[4,320,1,32]{1,3,2,0:T(8,128)(2,1)S(1)} %get-tuple-element.16), channel_id=1, source_target_pairs={{1,0},{2,1},{3,2},{5,4},{6,5},{7,6},{9,8},{10,9},{11,10},{13,12},{... | collective-permute-start | bytes 245768 | tf_op jit(solution)/shard_map/ppermute | solution.py:22
  7.3 0.5 iota_add_fusion
  7.8 0.0 collective-permute-done
  7.8 3.5 %collective-permute-done.1 = bf16[4,320,1,32]{1,3,2,0:T(8,128)(2,1)S(1)} collective-permute-done((bf16[4,320,1,32]{1,3,2,0:T(8,128)(2,1)S(1)}, bf16[4,320,1,32]{1,3,2,0:T(8,128)(2,1)S(1)}, u32[]{:S(2)}, u32[]{:S(2)}) %collective-permute-start.1) | collective-permute-done | bytes 81952 | tf_op jit(solution)/shard_map/ppermute | solution.py:22
  11.3 0.6 copy-done.4
  11.9 0.3 fusion.27
  12.2 2.3 %pad_maximum_fusion.3 = (bf16[4,320,4,32]{1,3,2,0:T(8,128)(2,1)S(1)}, bf16[4,320,4,32]{1,3,2,0:T(8,128)(2,1)S(1)}, bf16[4,320,4,32]{1,3,2,0:T(8,128)(2,1)S(1)}, ...) fusion(bf16[4,320,1,32]{1,3,2,0:T(8,128)(2,1)} %copy-done.4, ...), kind=kLoop, calls=%fused_computation.57 | loop fusion | flops 327680 | bytes 5079040 | tf_op jit(solution)/shard_map/concatenate | solution.py:18
  14.6 5.8 %concatenate.28 = bf16[4,2880,4,32]{1,3,2,0:T(8,128)(2,1)} concatenate(bf16[4,320,4,32]{1,3,2,0:T(8,128)(2,1)S(1)} %get-tuple-element.23, bf16[4,320,4,32]{1,3,2,0:T(8,128)(2,1)S(1)} %get-tuple-element.14, bf16[4,320,4,32]{1,3,2,0:T(8,128)(2,1)} %get-tuple-element.24, bf16[4,320,4,32]{1,3,2,0:T(8,128)(2,1)} %get-tuple-element.25, bf16[4,320,4,32]{1,3,2,0:T(8,128)(2,1)S(1)} %bitcast.73, ...), dimensions={1} | concatenate | bytes 5898240 | tf_op jit(solution)/shard_map/concatenate | solution.py:98
  20.4 0.0 copy-done
  20.4 4.5 %fusion.1 = f32[4,4,32,320]{3,2,1,0:T(8,128)} fusion(bf16[4,2880,4,32]{1,3,2,0:T(8,128)(2,1)} %concatenate.28, bf16[320,2880]{1,0:T(8,128)(2,1)S(1)} %copy-done), kind=kOutput, calls=%fused_computation.3 | convolution fusion | flops 943718400 | bytes 5447680 | tf_op jit(solution)/shard_map/oj,fjrw->forw/dot_general | solution.py:99
  25.0 1.5 %copy.16 = f32[4,320,128]{2,1,0:T(8,128)S(1)} copy(f32[4,320,128]{1,2,0:T(8,128)} %bitcast.78) | data formatting | bytes 1310720 | tf_op jit(solution)/shard_map/reshape | solution.py:101
  26.4 0.0 copy-done.3
  26.4 0.2 fusion.36
  26.6 3.1 %collective-permute-start.2 = (bf16[1,320,128]{2,1,0:T(8,128)(2,1)S(1)}, bf16[1,320,128]{2,1,0:T(8,128)(2,1)S(1)}, u32[]{:S(2)}, u32[]{:S(2)}) collective-permute-start(bf16[1,320,128]{2,1,0:T(8,128)(2,1)S(1)} %get-tuple-element.17), channel_id=1, source_target_pairs={{0,4},{4,8},{8,12},{12,16},{16,20},{20,24},{24,28},{28,32},{32,36}... | collective-permute-start | bytes 245768 | tf_op jit(solution)/shard_map/ppermute | solution.py:20
  29.8 4.3 %collective-permute-start.3 = (bf16[1,320,128]{2,1,0:T(8,128)(2,1)S(1)}, bf16[1,320,128]{2,1,0:T(8,128)(2,1)S(1)}, u32[]{:S(2)}, u32[]{:S(2)}) collective-permute-start(bf16[1,320,128]{2,1,0:T(8,128)(2,1)S(1)} %get-tuple-element.18), channel_id=1, source_target_pairs={{4,0},{8,4},{12,8},{16,12},{20,16},{24,20},{28,24},{32,28},{36,32}... | collective-permute-start | bytes 245768 | tf_op jit(solution)/shard_map/ppermute | solution.py:22
  34.1 0.0 copy-start.5
  34.1 0.0 collective-permute-done.2
  34.1 1.4 %collective-permute-done.3 = bf16[1,320,128]{2,1,0:T(8,128)(2,1)S(1)} collective-permute-done((bf16[1,320,128]{2,1,0:T(8,128)(2,1)S(1)}, bf16[1,320,128]{2,1,0:T(8,128)(2,1)S(1)}, u32[]{:S(2)}, u32[]{:S(2)}) %collective-permute-start.3) | collective-permute-done | bytes 81952 | tf_op jit(solution)/shard_map/ppermute | solution.py:22
  35.5 0.0 copy-done.10
  35.5 0.5 fusion.48
  36.0 0.0 copy-start.1
  36.0 0.0 copy-start.6
  36.1 0.1 multiply_reduce_fusion
  36.2 0.0 copy-start.9
  36.2 0.0 copy-start.11
  36.2 0.0 copy-start.8
  36.2 0.0 copy-start.7
  36.2 0.1 multiply_convert_fusion
  36.3 0.0 copy-done.5
  36.3 0.3 fusion.14
  36.6 0.6 copy-done.6
  37.2 0.3 fusion.15
  37.6 0.1 pad_maximum_fusion.2
  37.6 0.0 copy-done.1
  37.6 5.1 %collective-permute-start.4 = (bf16[4,2,320,128]{3,2,0,1:T(8,128)(2,1)S(1)}, bf16[4,2,320,128]{3,2,0,1:T(8,128)(2,1)}, u32[]{:S(2)}, u32[]{:S(2)}) collective-permute-start(bf16[4,2,320,128]{3,2,0,1:T(8,128)(2,1)S(1)} %pad_maximum_fusion.2), channel_id=1, source_target_pairs={{0,8},{4,12},{8,16},{12,20},{16,24},{20,28},{24,32},{28,36},{32,40... | collective-permute-start | bytes 1966088 | tf_op jit(solution)/shard_map/ppermute | solution.py:32
  42.8 0.0 copy-done.9
  42.8 0.1 broadcast_subtract_fusion
  42.9 6.1 %collective-permute-start.5 = (bf16[4,2,320,128]{3,2,0,1:T(8,128)(2,1)S(1)}, bf16[4,2,320,128]{3,2,0,1:T(8,128)(2,1)}, u32[]{:S(2)}, u32[]{:S(2)}) collective-permute-start(bf16[4,2,320,128]{3,2,0,1:T(8,128)(2,1)S(1)} %pad_maximum_fusion.2), channel_id=1, source_target_pairs={{0,4},{4,8},{8,12},{12,16},{16,20},{20,24},{24,28},{28,32},{32,36}... | collective-permute-start | bytes 1966088 | tf_op jit(solution)/shard_map/ppermute | solution.py:32
  48.9 0.0 copy-done.11
  49.0 1.9 %collective-permute-start.6 = (bf16[4,2,320,128]{3,2,0,1:T(8,128)(2,1)S(1)}, bf16[4,2,320,128]{3,2,0,1:T(8,128)(2,1)}, u32[]{:S(2)}, u32[]{:S(2)}) collective-permute-start(bf16[4,2,320,128]{3,2,0,1:T(8,128)(2,1)S(1)} %pad_maximum_fusion.2), channel_id=1, source_target_pairs={{4,0},{8,4},{12,8},{16,12},{20,16},{24,20},{28,24},{32,28},{36,32}... | collective-permute-start | bytes 1966088 | tf_op jit(solution)/shard_map/ppermute | solution.py:32
  50.9 0.1 and_and_fusion
  51.0 1.9 %collective-permute-start.7 = (bf16[4,2,320,128]{3,2,0,1:T(8,128)(2,1)S(1)}, bf16[4,2,320,128]{3,2,0,1:T(8,128)(2,1)}, u32[]{:S(2)}, u32[]{:S(2)}) collective-permute-start(bf16[4,2,320,128]{3,2,0,1:T(8,128)(2,1)S(1)} %pad_maximum_fusion.2), channel_id=1, source_target_pairs={{8,0},{12,4},{16,8},{20,12},{24,16},{28,20},{32,24},{36,28},{40,32... | collective-permute-start | bytes 1966088 | tf_op jit(solution)/shard_map/ppermute | solution.py:32
  52.9 0.3 convolution_convert_fusion.1
  53.3 1.3 %copy.18 = bf16[4,5,64,128]{2,0,3,1:T(4,128)(2,1)} copy(bf16[4,5,64,128]{3,2,1,0:T(8,128)(2,1)S(1)} %bitcast.76) | data formatting | bytes 655360 | tf_op jit(solution)/shard_map/reshape | solution.py:59
  54.6 3.1 %collective-permute-done.4 = bf16[4,2,320,128]{3,2,0,1:T(8,128)(2,1)} collective-permute-done((bf16[4,2,320,128]{3,2,0,1:T(8,128)(2,1)S(1)}, bf16[4,2,320,128]{3,2,0,1:T(8,128)(2,1)}, u32[]{:S(2)}, u32[]{:S(2)}) %collective-permute-start.4) | collective-permute-done | bytes 655392 | tf_op jit(solution)/shard_map/ppermute | solution.py:32
  57.7 1.1 constant_dynamic-update-slice_fusion.4
  58.8 13.4 %collective-permute-done.5 = bf16[4,2,320,128]{3,2,0,1:T(8,128)(2,1)} collective-permute-done((bf16[4,2,320,128]{3,2,0,1:T(8,128)(2,1)S(1)}, bf16[4,2,320,128]{3,2,0,1:T(8,128)(2,1)}, u32[]{:S(2)}, u32[]{:S(2)}) %collective-permute-start.5) | collective-permute-done | bytes 655392 | tf_op jit(solution)/shard_map/ppermute | solution.py:32
  72.2 1.2 constant_dynamic-update-slice_fusion.3
  73.4 0.1 constant_dynamic-update-slice_fusion.2
  73.5 29.7 %collective-permute-done.6 = bf16[4,2,320,128]{3,2,0,1:T(8,128)(2,1)} collective-permute-done((bf16[4,2,320,128]{3,2,0,1:T(8,128)(2,1)S(1)}, bf16[4,2,320,128]{3,2,0,1:T(8,128)(2,1)}, u32[]{:S(2)}, u32[]{:S(2)}) %collective-permute-start.6) | collective-permute-done | bytes 655392 | tf_op jit(solution)/shard_map/ppermute | solution.py:32
  103.3 1.2 constant_dynamic-update-slice_fusion.1
  104.4 0.0 collective-permute-done.7
  104.4 1.2 constant_dynamic-update-slice_fusion
  105.6 1.4 %fusion.44 = (bf16[20,1,320,128]{3,2,0,1:T(8,128)(2,1)}, bf16[20,1,320,128]{3,2,0,1:T(8,128)(2,1)S(1)}) fusion(bf16[20,2,320,128]{3,2,0,1:T(8,128)(2,1)S(1)} %constant_dynamic-update-slice_fusion), kind=kLoop, calls=%fused_computation.76 | loop fusion | bytes 6553600 | tf_op jit(solution)/shard_map/slice | solution.py:119
  107.1 5.4 %copy.17 = bf16[20,5,64,128]{2,0,3,1:T(8,128)(2,1)} copy(bf16[20,5,64,128]{3,2,1,0:T(8,128)(2,1)} %bitcast.75) | data formatting | bytes 3276800 | tf_op jit(solution)/shard_map/reshape;squeeze | solution.py:60
  112.5 3.8 %copy.19 = bf16[20,5,64,128]{2,0,3,1:T(8,128)(2,1)} copy(bf16[20,5,64,128]{3,2,1,0:T(8,128)(2,1)S(1)} %bitcast.74) | data formatting | bytes 3276800 | tf_op jit(solution)/shard_map/reshape;squeeze | solution.py:61
  116.3 5.7 %fusion.49 = (f32[4,5,128]{0,2,1:T(8,128)S(1)}, f32[4,20,5,128]{1,0,3,2:T(4,128)}) fusion(bf16[20,5,64,128]{2,0,3,1:T(8,128)(2,1)} %copy.17, bf16[4,5,64,128]{2,0,3,1:T(4,128)(2,1)} %copy.18, pred[4,20,5]{1,0,2:T(4,128)(4,1)S(1)} %and_and_fusion), kind=kOutput, calls=%fused_computation.81 | convolution fusion | flops 6758419 | bytes 2181520 | tf_op jit(solution)/shard_map/sub | solution.py:76
  122.0 3.9 %fusion.8 = bf16[4,5,64,128]{2,0,3,1:T(4,128)(2,1)S(1)} fusion(bf16[20,5,64,128]{2,0,3,1:T(8,128)(2,1)} %copy.19, f32[4,20,5,128]{1,0,3,2:T(4,128)} %get-tuple-element.22, f32[4,5,128]{0,2,1:T(8,128)S(1)} %get-tuple-element.21), kind=kOutput, calls=%fused_computation.13 | convolution fusion | flops 6819840 | bytes 2181120 | tf_op jit(solution)/shard_map/tshp,shdp->thdp/dot_general | solution.py:78
  125.9 0.9 copy.20
  126.8 2.0 %fusion.11 = bf16[4,320,128]{2,1,0:T(8,128)(2,1)} fusion(f32[4,320,128]{2,1,0:T(8,128)S(1)} %copy-done.2, bf16[4,320,128]{2,1,0:T(8,128)(2,1)S(1)} %bitcast.77, bf16[320,320]{1,0:T(8,128)(2,1)} %param.15), kind=kOutput, calls=%fused_computation.18 | convolution fusion | flops 105185280 | bytes 1515520 | tf_op jit(solution)/shard_map/oi,fip->fop/dot_general | solution.py:133
  (14 shorter events, 0.1 us)
Async XLA Ops:
  0.0 20.4 %copy-start = (bf16[320,2880]{1,0:T(8,128)(2,1)S(1)}, bf16[320,2880]{1,0:T(8,128)(2,1)}, u32[]{:S(2)}) copy-start(bf16[320,2880]{1,0:T(8,128)(2,1)} %param.10) | copy-start | bytes 5529604
  1.6 6.2 %collective-permute-start = (bf16[4,320,1,32]{1,3,2,0:T(8,128)(2,1)S(1)}, bf16[4,320,1,32]{1,3,2,0:T(8,128)(2,1)S(1)}, u32[]{:S(2)}, u32[]{:S(2)}) collective-permute-start(bf16[4,320,1,32]{1,3,2,0:T(8,128)(2,1)S(1)} %get-tuple-element.15), channel_id=1, source_target_pairs={{0,1},{1,2},{2,3},{4,5},{5,6},{6,7},{8,9},{9,10},{10,11},{12,13},{... | collective-permute-start | bytes 245768 | tf_op jit(solution)/shard_map/ppermute | solution.py:20
  5.3 5.9 %collective-permute-start.1 = (bf16[4,320,1,32]{1,3,2,0:T(8,128)(2,1)S(1)}, bf16[4,320,1,32]{1,3,2,0:T(8,128)(2,1)S(1)}, u32[]{:S(2)}, u32[]{:S(2)}) collective-permute-start(bf16[4,320,1,32]{1,3,2,0:T(8,128)(2,1)S(1)} %get-tuple-element.16), channel_id=1, source_target_pairs={{1,0},{2,1},{3,2},{5,4},{6,5},{7,6},{9,8},{10,9},{11,10},{13,12},{... | collective-permute-start | bytes 245768 | tf_op jit(solution)/shard_map/ppermute | solution.py:22
  11.3 0.6 copy-start.4
  20.4 6.0 %copy-start.3 = (bf16[4,320,128]{2,1,0:T(8,128)(2,1)S(1)}, bf16[4,320,128]{2,1,0:T(8,128)(2,1)}, u32[]{:S(2)}) copy-start(bf16[4,320,128]{2,1,0:T(8,128)(2,1)} %param.9) | copy-start | bytes 983044
  25.0 10.6 %copy-start.10 = (bf16[320,960]{1,0:T(8,128)(2,1)S(1)}, bf16[320,960]{1,0:T(8,128)(2,1)}, u32[]{:S(2)}) copy-start(bf16[320,960]{1,0:T(8,128)(2,1)} %param.11) | copy-start | bytes 1843204
  26.6 7.4 %collective-permute-start.2 = (bf16[1,320,128]{2,1,0:T(8,128)(2,1)S(1)}, bf16[1,320,128]{2,1,0:T(8,128)(2,1)S(1)}, u32[]{:S(2)}, u32[]{:S(2)}) collective-permute-start(bf16[1,320,128]{2,1,0:T(8,128)(2,1)S(1)} %get-tuple-element.17), channel_id=1, source_target_pairs={{0,4},{4,8},{8,12},{12,16},{16,20},{20,24},{24,28},{28,32},{32,36}... | collective-permute-start | bytes 245768 | tf_op jit(solution)/shard_map/ppermute | solution.py:20
  29.8 5.7 %collective-permute-start.3 = (bf16[1,320,128]{2,1,0:T(8,128)(2,1)S(1)}, bf16[1,320,128]{2,1,0:T(8,128)(2,1)S(1)}, u32[]{:S(2)}, u32[]{:S(2)}) collective-permute-start(bf16[1,320,128]{2,1,0:T(8,128)(2,1)S(1)} %get-tuple-element.18), channel_id=1, source_target_pairs={{4,0},{8,4},{12,8},{16,12},{20,16},{24,20},{28,24},{32,28},{36,32}... | collective-permute-start | bytes 245768 | tf_op jit(solution)/shard_map/ppermute | solution.py:22
  34.1 2.2 %copy-start.5 = (bf16[320,320]{1,0:T(8,128)(2,1)S(1)}, bf16[320,320]{1,0:T(8,128)(2,1)}, u32[]{:S(2)}) copy-start(bf16[320,320]{1,0:T(8,128)(2,1)} %param.13) | copy-start | bytes 614404
  36.0 1.6 %copy-start.1 = (f32[4,320,128]{2,1,0:T(8,128)}, f32[4,320,128]{2,1,0:T(8,128)S(1)}, u32[]{:S(2)}) copy-start(f32[4,320,128]{2,1,0:T(8,128)S(1)} %get-tuple-element.20) | copy-start | bytes 1966084
  36.0 1.2 copy-start.6
  36.2 6.6 %copy-start.9 = (s32[4]{0:T(128)S(1)}, s32[4]{0:T(128)}, u32[]{:S(2)}) copy-start(s32[4]{0:T(128)} %iota_add_fusion) | copy-start | bytes 52
  36.2 12.8 %copy-start.11 = (s32[5]{0:T(128)S(1)}, s32[5]{0:T(128)}, u32[]{:S(2)}) copy-start(s32[5]{0:T(128)} %param.16) | copy-start | bytes 64
  36.2 14.7 %copy-start.8 = (s32[5]{0:T(128)S(1)}, s32[5]{0:T(128)}, u32[]{:S(2)}) copy-start(s32[5]{0:T(128)} %param.17) | copy-start | bytes 64
  36.2 16.7 %copy-start.7 = (bf16[320,320]{1,0:T(8,128)(2,1)S(1)}, bf16[320,320]{1,0:T(8,128)(2,1)}, u32[]{:S(2)}) copy-start(bf16[320,320]{1,0:T(8,128)(2,1)} %param.12) | copy-start | bytes 614404
  37.6 20.1 %collective-permute-start.4 = (bf16[4,2,320,128]{3,2,0,1:T(8,128)(2,1)S(1)}, bf16[4,2,320,128]{3,2,0,1:T(8,128)(2,1)}, u32[]{:S(2)}, u32[]{:S(2)}) collective-permute-start(bf16[4,2,320,128]{3,2,0,1:T(8,128)(2,1)S(1)} %pad_maximum_fusion.2), channel_id=1, source_target_pairs={{0,8},{4,12},{8,16},{12,20},{16,24},{20,28},{24,32},{28,36},{32,40... | collective-permute-start | bytes 1966088 | tf_op jit(solution)/shard_map/ppermute | solution.py:32
  42.9 29.4 %collective-permute-start.5 = (bf16[4,2,320,128]{3,2,0,1:T(8,128)(2,1)S(1)}, bf16[4,2,320,128]{3,2,0,1:T(8,128)(2,1)}, u32[]{:S(2)}, u32[]{:S(2)}) collective-permute-start(bf16[4,2,320,128]{3,2,0,1:T(8,128)(2,1)S(1)} %pad_maximum_fusion.2), channel_id=1, source_target_pairs={{0,4},{4,8},{8,12},{12,16},{16,20},{20,24},{24,28},{28,32},{32,36}... | collective-permute-start | bytes 1966088 | tf_op jit(solution)/shard_map/ppermute | solution.py:32
  49.0 54.3 %collective-permute-start.6 = (bf16[4,2,320,128]{3,2,0,1:T(8,128)(2,1)S(1)}, bf16[4,2,320,128]{3,2,0,1:T(8,128)(2,1)}, u32[]{:S(2)}, u32[]{:S(2)}) collective-permute-start(bf16[4,2,320,128]{3,2,0,1:T(8,128)(2,1)S(1)} %pad_maximum_fusion.2), channel_id=1, source_target_pairs={{4,0},{8,4},{12,8},{16,12},{20,16},{24,20},{28,24},{32,28},{36,32}... | collective-permute-start | bytes 1966088 | tf_op jit(solution)/shard_map/ppermute | solution.py:32
  51.0 53.4 %collective-permute-start.7 = (bf16[4,2,320,128]{3,2,0,1:T(8,128)(2,1)S(1)}, bf16[4,2,320,128]{3,2,0,1:T(8,128)(2,1)}, u32[]{:S(2)}, u32[]{:S(2)}) collective-permute-start(bf16[4,2,320,128]{3,2,0,1:T(8,128)(2,1)S(1)} %pad_maximum_fusion.2), channel_id=1, source_target_pairs={{8,0},{12,4},{16,8},{20,12},{24,16},{28,20},{32,24},{36,28},{40,32... | collective-permute-start | bytes 1966088 | tf_op jit(solution)/shard_map/ppermute | solution.py:32
  122.0 4.8 %copy-start.2 = (f32[4,320,128]{2,1,0:T(8,128)S(1)}, f32[4,320,128]{2,1,0:T(8,128)}, u32[]{:S(2)}) copy-start(f32[4,320,128]{2,1,0:T(8,128)} %copy-done.1) | copy-start | bytes 1966084
where the time goes:
time: 130 us; the launch traced here: 129 us
  waiting for transfers between devices  51.2 us (39%)
  starting transfers between devices  28.1 us (22%)
  local copies, waits for them, and re-layouts  26.3 us (20%)
  matrix products  17.7 us (14%)
  other arithmetic  5.17 us (4%)
    ppermute x4, waiting for transfers between devices, shifted(): lax.ppermute(value, axis, [(source, source + steps) for source in range(l...  46.3 us
    ppermute x4, starting transfers between devices, shifted(): lax.ppermute(value, axis, [(source, source + steps) for source in range(l...  15 us
    ppermute x2, starting transfers between devices, padded_2(): lax.ppermute(tail, axis, [(i, (i + 1) % count) for i in range(ends)])  6.89 us
    ppermute x2, starting transfers between devices, padded_2(): lax.ppermute(head, axis, [((i + 1) % count, i) for i in range(ends)])  6.19 us
    concatenate x1, local copies, waits for them, and re-layouts, per_device(): stacked = jnp.concatenate(tap_list, axis=1)  5.84 us
    sub x1, matrix products, attend(): raised = jnp.exp(masked - highest)  5.68 us
    another operation x1, local copies, waits for them, and re-layouts, attend(): key_heads = key_frames.reshape(key_count, HEADS, HEAD_DIM, cell_count)  5.42 us
    ppermute x2, waiting for transfers between devices, padded_2(): lax.ppermute(head, axis, [((i + 1) % count, i) for i in range(ends)])  4.89 us
  transfers between devices with their start and end apart: 8, of which 5 were waited for; matrix products, arithmetic and copies ran while one was open for 5% of the time, Pallas kernels for 0%

commit v1 on v0

v1 whole, which is shorter than its diff:
```python
import functools

import jax
import jax.numpy as jnp
from jax import lax
from jax.experimental import pallas as pl
from jax.experimental.pallas import tpu as pltpu
from jax.sharding import PartitionSpec as P

HEADS = 5
HEAD_DIM = 64
WIDE = 32
WMAX = 8
C = 320
F = 4
LANES = 128
MESH = pl.DeviceIdType.MESH
F32 = jnp.float32
BF16 = jnp.bfloat16
PAIRS = ((0, 3), (1, 2))
ORDER = (1, 2, 0, 3)


def silu(v):
    return 0.5 * v * (1.0 + jnp.tanh(0.5 * v))


def roll(v, shift):
    shift = shift % LANES
    return v if shift == 0 else pltpu.roll(v, shift, 1)


def kernel(
    frame_total,
    wl_ref,
    wr_ref,
    x_hbm,
    cs_hbm,
    ct_hbm,
    wq_hbm,
    wk_hbm,
    wv_hbm,
    wo_hbm,
    out_ref,
    x_ref,
    cs_ref,
    ct_ref,
    wqkv_ref,
    wo_ref,
    hsend,
    hrecv,
    active_ref,
    xcol,
    part_ref,
    settled_ref,
    moving_ref,
    stream_ref,
    near_ref,
    q_ref,
    k_ref,
    v_ref,
    acc_ref,
    m_ref,
    l_ref,
    load_sem,
    hs_sem,
    hr_sem,
    ts_sem,
    tr_sem,
    gs_sem,
    gr_sem,
):
    nt = lax.axis_size("tm")
    nh = lax.axis_size("height")
    it = lax.axis_index("tm")
    ih = lax.axis_index("height")
    t_next, t_prev = lax.rem(it + 1, nt), lax.rem(it + nt - 1, nt)
    h_next, h_prev = lax.rem(ih + 1, nh), lax.rem(ih + nh - 1, nh)

    loads = []
    for n, (src, dst) in enumerate(
        (
            (x_hbm, x_ref),
            (cs_hbm, cs_ref),
            (ct_hbm, ct_ref),
            (wq_hbm, wqkv_ref.at[pl.ds(0, C)]),
            (wk_hbm, wqkv_ref.at[pl.ds(C, C)]),
            (wv_hbm, wqkv_ref.at[pl.ds(2 * C, C)]),
            (wo_hbm, wo_ref),
        )
    ):
        copy = pltpu.make_async_copy(src, dst, load_sem.at[n])
        copy.start()
        loads.append(copy)

    barrier = pltpu.get_barrier_semaphore()
    for dev in ((t_next, ih), (t_prev, ih), (it, h_next), (it, h_prev)):
        pl.semaphore_signal(barrier, inc=1, device_id=dev, device_id_type=MESH)

    def remote(src, dst, ssem, rsem, dev):
        return pltpu.make_async_remote_copy(
            src_ref=src, dst_ref=dst, send_sem=ssem, recv_sem=rsem, device_id=dev, device_id_type=MESH
        )

    lane = lax.broadcasted_iota(jnp.int32, (C, LANES), 1)
    col = jnp.bitwise_and(lane, WIDE - 1)
    group = lax.shift_right_logical(lane, 5)

    loads[0].wait()
    top = jnp.zeros((C, LANES), F32)
    bottom = jnp.zeros((C, LANES), F32)
    for f in range(F):
        act = silu(x_ref[f].astype(F32))
        active_ref[f] = act
        top = jnp.where(group == f, roll(act, WIDE * f), top)
        bottom = jnp.where(group == f, roll(act, WIDE * f - 96), bottom)
    hsend[0] = bottom.astype(BF16)
    hsend[1] = top.astype(BF16)
    pl.semaphore_wait(barrier, 4)
    row_down = remote(hsend.at[0], hrecv.at[0], hs_sem.at[0], hr_sem.at[0], (it, h_next))
    row_up = remote(hsend.at[1], hrecv.at[1], hs_sem.at[1], hr_sem.at[1], (it, h_prev))
    row_down.start()
    row_up.start()

    def fill(n, k, a, rows):
        lanes = pl.ds(LANES * k, LANES)
        base = 3 * a * C
        xcol[n, pl.ds(base, C), lanes] = jnp.where(col == 0, 0.0, roll(rows, 1)).astype(BF16)
        xcol[n, pl.ds(base + C, C), lanes] = rows.astype(BF16)
        xcol[n, pl.ds(base + 2 * C, C), lanes] = jnp.where(col == WIDE - 1, 0.0, roll(rows, -1)).astype(BF16)

    for n in range(2):
        for k, f in enumerate(PAIRS[n]):
            fill(n, k, 1, active_ref[f])
    loads[1].wait()
    for n in range(2):
        part_ref[n] = jnp.dot(
            cs_ref[:, 1024:1920], xcol[n, pl.ds(1024, 896), :], preferred_element_type=F32
        )

    row_down.wait_recv()
    row_up.wait_recv()
    above = jnp.where(ih > 0, hrecv[0].astype(F32), 0.0)
    below = jnp.where(ih < nh - 1, hrecv[1].astype(F32), 0.0)

    def settle(n):
        for k, f in enumerate(PAIRS[n]):
            act = active_ref[f]
            fill(n, k, 0, jnp.where(group == 0, roll(above, -WIDE * f), roll(act, WIDE)))
            fill(n, k, 2, jnp.where(group == 3, roll(below, 96 - WIDE * f), roll(act, -WIDE)))
        total = part_ref[n]
        total += jnp.dot(cs_ref[:, 0:1024], xcol[n, pl.ds(0, 1024), :], preferred_element_type=F32)
        total += jnp.dot(cs_ref[:, 1920:2880], xcol[n, pl.ds(1920, 960), :], preferred_element_type=F32)
        for k, f in enumerate(PAIRS[n]):
            settled = (x_ref[f].astype(F32) + total[:, LANES * k : LANES * (k + 1)]).astype(BF16)
            settled_ref[f] = settled
            moving_ref[f + 1] = silu(settled.astype(F32)).astype(BF16)

    settle(0)
    to_next = remote(moving_ref.at[F], moving_ref.at[0], ts_sem.at[0], tr_sem.at[0], (t_next, ih))
    to_prev = remote(moving_ref.at[1], moving_ref.at[F + 1], ts_sem.at[1], tr_sem.at[1], (t_prev, ih))
    to_next.start()
    to_prev.start()
    settle(1)

    def gather(step, direction):
        f = ORDER[step % F]
        if direction == 0:
            src = 8 + f if step < F else 4 + f
            dst, dev = src - 4, (t_next, ih)
        else:
            src = 8 + f if step < F else 12 + f
            dst, dev = src + 4, (t_prev, ih)
        return remote(
            near_ref.at[src], near_ref.at[dst], gs_sem.at[direction, step], gr_sem.at[direction, step], dev
        )

    def temporal(n):
        stacked = jnp.concatenate(
            [moving_ref[pl.ds(f, 3)].reshape(3 * C, LANES) for f in PAIRS[n]], axis=1
        )
        total = jnp.dot(ct_ref[...], stacked, preferred_element_type=F32)
        for k, f in enumerate(PAIRS[n]):
            stream = (settled_ref[f].astype(F32) + total[:, LANES * k : LANES * (k + 1)]).astype(BF16)
            stream_ref[f] = stream
            wide = stream.astype(F32)
            centred = wide - jnp.sum(wide, axis=0, keepdims=True) * (1.0 / C)
            spread = jnp.sum(centred * centred, axis=0, keepdims=True) * (1.0 / C)
            near_ref[8 + f] = (centred * lax.rsqrt(spread + 1e-05)).astype(BF16)

    loads[2].wait()
    temporal(1)
    copies = {}
    for step in (0, 1):
        for direction in (0, 1):
            copies[step, direction] = gather(step, direction)
            copies[step, direction].start()
    to_next.wait_recv()
    to_prev.wait_recv()

    @pl.when(it == 0)
    def _():
        moving_ref[0] = jnp.zeros((C, LANES), BF16)

    @pl.when(it == nt - 1)
    def _():
        moving_ref[F + 1] = jnp.zeros((C, LANES), BF16)

    temporal(0)
    for step in (2, 3):
        for direction in (0, 1):
            copies[step, direction] = gather(step, direction)
            copies[step, direction].start()

    for n in (3, 4, 5):
        loads[n].wait()

    def joined(first):
        return jnp.concatenate([near_ref[first + f] for f in range(F)], axis=1)

    own = joined(8)
    made = jnp.dot(wqkv_ref[pl.ds(0, C)], own, preferred_element_type=F32)
    for f in range(F):
        q_ref[f] = (made[:, LANES * f : LANES * (f + 1)]).astype(BF16)

    def keys(first):
        near = joined(first)
        made = jnp.dot(wqkv_ref[pl.ds(C, 2 * C)], near, preferred_element_type=F32)
        for f in range(F):
            part = made[:, LANES * f : LANES * (f + 1)].astype(BF16)
            k_ref[f] = part[:C]
            v_ref[f] = part[C:]

    head_row = lax.broadcasted_iota(jnp.int32, (8, LANES), 0)
    reach_left = jnp.zeros((8, LANES), jnp.int32)
    reach_right = jnp.zeros((8, LANES), jnp.int32)
    for h in range(HEADS):
        reach_left = jnp.where(head_row == h, wl_ref[h], reach_left)
        reach_right = jnp.where(head_row == h, wr_ref[h], reach_right)
    summing = jnp.where(
        lax.shift_right_logical(lax.broadcasted_iota(jnp.int32, (16, C), 1), 6)
        == lax.broadcasted_iota(jnp.int32, (16, C), 0),
        1.0,
        0.0,
    ).astype(BF16)

    def attend(first, fresh):
        keys(first)

        def step(t, carry):
            query = q_ref[t]
            products = jnp.concatenate([query * k_ref[s] for s in range(F)], axis=1)
            scores = jnp.dot(summing, products, preferred_element_type=F32)[:8] * HEAD_DIM ** (-0.5)
            masked = []
            for s in range(F):
                offset = first - 8 + s - t
                position = F * it + (first - 8 + s)
                inside = (position >= 0) & (position < frame_total)
                far = jnp.where(inside, offset, 2 * WMAX + F)
                allowed = (far >= -reach_left) & (far <= reach_right)
                masked.append(jnp.where(allowed, scores[:, LANES * s : LANES * (s + 1)], -1e30))
            highest = jnp.maximum(jnp.maximum(masked[0], masked[1]), jnp.maximum(masked[2], masked[3]))
            if not fresh:
                before = m_ref[t]
                highest = jnp.maximum(highest, before)
                fade = jnp.exp(before - highest)
            raised = [jnp.exp(one - highest) for one in masked]
            total = (raised[0] + raised[1]) + (raised[2] + raised[3])
            if not fresh:
                total = total + l_ref[t] * fade
            m_ref[t] = highest
            l_ref[t] = total
            for h in range(HEADS):
                rows = pl.ds(HEAD_DIM * h, HEAD_DIM)
                acc = raised[0][h : h + 1] * v_ref[0, rows].astype(F32)
                for s in range(1, F):
                    acc += raised[s][h : h + 1] * v_ref[s, rows].astype(F32)
                if not fresh:
                    acc += acc_ref[t, rows] * fade[h : h + 1]
                acc_ref[t, rows] = acc
            return carry

        lax.fori_loop(0, F, step, 0)

    attend(8, True)

    for step in range(F):
        for direction in (0, 1):
            copies[step, direction].wait_recv()
            copies[step + F, direction] = gather(step + F, direction)
            copies[step + F, direction].start()
    attend(4, False)
    attend(12, False)
    for step in range(F, 2 * F):
        copies[step, 0].wait_recv()
    attend(0, False)
    for step in range(F, 2 * F):
        copies[step, 1].wait_recv()
    attend(16, False)

    loads[6].wait()
    blended = []
    for t in range(F):
        scale = 1.0 / l_ref[t]
        blended.append(
            jnp.concatenate(
                [
                    (acc_ref[t, pl.ds(HEAD_DIM * h, HEAD_DIM)] * scale[h : h + 1]).astype(BF16)
                    for h in range(HEADS)
                ],
                axis=0,
            )
        )
    mixed = jnp.dot(wo_ref[...], jnp.concatenate(blended, axis=1), preferred_element_type=F32)
    for t in range(F):
        out_ref[t] = (stream_ref[t].astype(F32) + mixed[:, LANES * t : LANES * (t + 1)]).astype(BF16)

    row_down.wait_send()
    row_up.wait_send()
    to_next.wait_send()
    to_prev.wait_send()
    for step in range(2 * F):
        for direction in (0, 1):
            copies[step, direction].wait_send()


def per_device(
    frames_in, conv_spatial, conv_temporal, w_query, w_key, w_value, w_out, win_left, win_right
):
    smem = pl.BlockSpec(memory_space=pltpu.SMEM)
    hbm = pl.BlockSpec(memory_space=pl.ANY)
    frame_total = F * lax.axis_size("tm")
    frame = (C, LANES)
    return pl.pallas_call(
        functools.partial(kernel, frame_total),
        out_shape=jax.ShapeDtypeStruct(frames_in.shape, BF16),
        in_specs=[smem, smem] + [hbm] * 7,
        out_specs=pl.BlockSpec(memory_space=pltpu.VMEM),
        scratch_shapes=[
            pltpu.VMEM((F,) + frame, BF16),
            pltpu.VMEM((C, 9 * C), BF16),
            pltpu.VMEM((C, 3 * C), BF16),
            pltpu.VMEM((3 * C, C), BF16),
            pltpu.VMEM((C, C), BF16),
            pltpu.VMEM((2,) + frame, BF16),
            pltpu.VMEM((2,) + frame, BF16),
            pltpu.VMEM((F,) + frame, F32),
            pltpu.VMEM((2, 9 * C, 2 * LANES), BF16),
            pltpu.VMEM((2, C, 2 * LANES), F32),
            pltpu.VMEM((F,) + frame, BF16),
            pltpu.VMEM((F + 2,) + frame, BF16),
            pltpu.VMEM((F,) + frame, BF16),
            pltpu.VMEM((F + 2 * WMAX,) + frame, BF16),
            pltpu.VMEM((F,) + frame, BF16),
            pltpu.VMEM((F,) + frame, BF16),
            pltpu.VMEM((F,) + frame, BF16),
            pltpu.VMEM((F,) + frame, F32),
            pltpu.VMEM((F, 8, LANES), F32),
            pltpu.VMEM((F, 8, LANES), F32),
            pltpu.SemaphoreType.DMA((7,)),
            pltpu.SemaphoreType.DMA((2,)),
            pltpu.SemaphoreType.DMA((2,)),
            pltpu.SemaphoreType.DMA((2,)),
            pltpu.SemaphoreType.DMA((2,)),
            pltpu.SemaphoreType.DMA((2, 2 * F)),
            pltpu.SemaphoreType.DMA((2, 2 * F)),
        ],
        compiler_params=pltpu.CompilerParams(
            collective_id=0, has_side_effects=True, vmem_limit_bytes=48 * 1024 * 1024
        ),
    )(win_left, win_right, frames_in, conv_spatial, conv_temporal, w_query, w_key, w_value, w_out)


def solution(mesh):
    return jax.shard_map(
        per_device,
        mesh=mesh,
        in_specs=(P("tm", None, "height"), P(), P(), P(), P(), P(), P(), P(), P()),
        out_specs=P("tm", None, "height"),
        check_vma=False,
    )
```

time: 130 us -> 58.2 us (0.45)
  the two profiles are of different devices: /device:TPU:97 before, /device:TPU:1 now
where the time goes in v1:
time: 58.2 us; the launch traced here: 57.8 us
  Pallas kernels  48.4 us (83%)
  local copies, waits for them, and re-layouts  9.39 us (16%)
    pallas_call x1, Pallas kernels, per_device(): pl.pallas_call(functools.partial(kernel, frame_total), out_shape=jax.Shap...  48.4 us
    unnamed x19, local copies, waits for them, and re-layouts  9.39 us

profile of v1, /device:TPU:1, one launch (start us, length us, event | category | flops | bytes accessed | tf_op | source)
XLA Modules:
  0.0 57.8 jit_solution(5563352227239574692)
XLA Ops:
  0.0 0.0 copy-start
  0.0 1.5 %copy-done = bf16[320,2880]{1,0:T(8,128)(2,1)S(1)} copy-done((bf16[320,2880]{1,0:T(8,128)(2,1)S(1)}, bf16[320,2880]{1,0:T(8,128)(2,1)}, u32[]{:S(2)}) %copy-start) | copy-done | bytes 1843224
  1.5 0.0 copy-start.1
  1.5 1.1 %copy-done.1 = bf16[320,960]{1,0:T(8,128)(2,1)S(1)} copy-done((bf16[320,960]{1,0:T(8,128)(2,1)S(1)}, bf16[320,960]{1,0:T(8,128)(2,1)}, u32[]{:S(2)}) %copy-start.1) | copy-done | bytes 614424
  2.6 0.0 copy-start.2
  2.6 1.0 %copy-done.2 = bf16[4,320,128]{2,1,0:T(8,128)(2,1)S(1)} copy-done((bf16[4,320,128]{2,1,0:T(8,128)(2,1)S(1)}, bf16[4,320,128]{2,1,0:T(8,128)(2,1)}, u32[]{:S(2)}) %copy-start.2) | copy-done | bytes 327704
  3.6 0.0 copy-start.3
  3.6 0.9 %copy-done.3 = bf16[320,320]{1,0:T(8,128)(2,1)S(1)} copy-done((bf16[320,320]{1,0:T(8,128)(2,1)S(1)}, bf16[320,320]{1,0:T(8,128)(2,1)}, u32[]{:S(2)}) %copy-start.3) | copy-done | bytes 204824
  4.5 0.0 copy-start.4
  4.5 0.9 %copy-done.4 = bf16[320,320]{1,0:T(8,128)(2,1)S(1)} copy-done((bf16[320,320]{1,0:T(8,128)(2,1)S(1)}, bf16[320,320]{1,0:T(8,128)(2,1)}, u32[]{:S(2)}) %copy-start.4) | copy-done | bytes 204824
  5.5 0.0 copy-start.5
  5.5 0.9 %copy-done.5 = bf16[320,320]{1,0:T(8,128)(2,1)S(1)} copy-done((bf16[320,320]{1,0:T(8,128)(2,1)S(1)}, bf16[320,320]{1,0:T(8,128)(2,1)}, u32[]{:S(2)}) %copy-start.5) | copy-done | bytes 204824
  6.4 0.0 copy-start.6
  6.4 0.9 %copy-done.6 = bf16[320,320]{1,0:T(8,128)(2,1)S(1)} copy-done((bf16[320,320]{1,0:T(8,128)(2,1)S(1)}, bf16[320,320]{1,0:T(8,128)(2,1)}, u32[]{:S(2)}) %copy-start.6) | copy-done | bytes 204824
  7.4 0.0 copy-start.7
  7.4 0.7 %copy-done.7 = s32[5]{0:T(128)S(1)} copy-done((s32[5]{0:T(128)S(1)}, s32[5]{0:T(128)}, u32[]{:S(2)}) %copy-start.7) | copy-done | bytes 44
  8.0 0.0 copy-start.8
  8.0 0.7 %copy-done.8 = s32[5]{0:T(128)S(1)} copy-done((s32[5]{0:T(128)S(1)}, s32[5]{0:T(128)}, u32[]{:S(2)}) %copy-start.8) | copy-done | bytes 44
  8.7 48.4 %shard_map.91 = bf16[4,320,128]{2,1,0:T(8,128)(2,1)S(1)} custom-call(s32[5]{0:T(128)S(1)} %copy-done.7, s32[5]{0:T(128)S(1)} %copy-done.8, bf16[4,320,128]{2,1,0:T(8,128)(2,1)S(1)} %copy-done.2, bf16[320,2880]{1,0:T(8,128)(2,1)S(1)} %copy-done, bf16[320,960]{1,0:T(8,128)(2,1)S(1)} %copy-done.1, bf16[320,320]{1,0:T(8,128)(2,1)S(1)} %copy-done.3, ...), custom_call_target="tpu_custom_call" | custom-call | tf_op jit(solution)/shard_map/pallas_call | solution.py:334
  57.1 0.7 %copy.11 = bf16[4,320,128]{2,1,0:T(8,128)(2,1)} copy(bf16[4,320,128]{2,1,0:T(8,128)(2,1)S(1)} %shard_map.91) | data formatting | bytes 655360
Async XLA Ops:
  0.0 1.5 %copy-start = (bf16[320,2880]{1,0:T(8,128)(2,1)S(1)}, bf16[320,2880]{1,0:T(8,128)(2,1)}, u32[]{:S(2)}) copy-start(bf16[320,2880]{1,0:T(8,128)(2,1)} %cs_hbm.1) | copy-start | bytes 5529604
  1.5 1.1 %copy-start.1 = (bf16[320,960]{1,0:T(8,128)(2,1)S(1)}, bf16[320,960]{1,0:T(8,128)(2,1)}, u32[]{:S(2)}) copy-start(bf16[320,960]{1,0:T(8,128)(2,1)} %ct_hbm.1) | copy-start | bytes 1843204
  2.6 1.0 %copy-start.2 = (bf16[4,320,128]{2,1,0:T(8,128)(2,1)S(1)}, bf16[4,320,128]{2,1,0:T(8,128)(2,1)}, u32[]{:S(2)}) copy-start(bf16[4,320,128]{2,1,0:T(8,128)(2,1)} %x_hbm.1) | copy-start | bytes 983044
  3.6 0.9 %copy-start.3 = (bf16[320,320]{1,0:T(8,128)(2,1)S(1)}, bf16[320,320]{1,0:T(8,128)(2,1)}, u32[]{:S(2)}) copy-start(bf16[320,320]{1,0:T(8,128)(2,1)} %wq_hbm.1) | copy-start | bytes 614404
  4.5 0.9 %copy-start.4 = (bf16[320,320]{1,0:T(8,128)(2,1)S(1)}, bf16[320,320]{1,0:T(8,128)(2,1)}, u32[]{:S(2)}) copy-start(bf16[320,320]{1,0:T(8,128)(2,1)} %wk_hbm.1) | copy-start | bytes 614404
  5.5 0.9 %copy-start.5 = (bf16[320,320]{1,0:T(8,128)(2,1)S(1)}, bf16[320,320]{1,0:T(8,128)(2,1)}, u32[]{:S(2)}) copy-start(bf16[320,320]{1,0:T(8,128)(2,1)} %wv_hbm.1) | copy-start | bytes 614404
  6.4 0.9 %copy-start.6 = (bf16[320,320]{1,0:T(8,128)(2,1)S(1)}, bf16[320,320]{1,0:T(8,128)(2,1)}, u32[]{:S(2)}) copy-start(bf16[320,320]{1,0:T(8,128)(2,1)} %wo_hbm.1) | copy-start | bytes 614404
  7.4 0.7 %copy-start.7 = (s32[5]{0:T(128)S(1)}, s32[5]{0:T(128)}, u32[]{:S(2)}) copy-start(s32[5]{0:T(128)} %wl_ref.1) | copy-start | bytes 64
  8.0 0.7 %copy-start.8 = (s32[5]{0:T(128)S(1)}, s32[5]{0:T(128)}, u32[]{:S(2)}) copy-start(s32[5]{0:T(128)} %wr_ref.1) | copy-start | bytes 64

commit v2 on v1

v2 whole, which is shorter than its diff:
```python
import functools

import jax
import jax.numpy as jnp
from jax import lax
from jax.experimental import pallas as pl
from jax.experimental.pallas import tpu as pltpu
from jax.sharding import PartitionSpec as P

HEADS = 5
HEAD_DIM = 64
WIDE = 32
C = 320
F = 4
LANES = 128
MESH = pl.DeviceIdType.MESH
F32 = jnp.float32
BF16 = jnp.bfloat16
PAIRS = ((0, 3), (1, 2))


def silu(v):
    return 0.5 * v * (1.0 + jnp.tanh(0.5 * v))


def roll(v, shift):
    shift = shift % LANES
    return v if shift == 0 else pltpu.roll(v, shift, 1)


def kernel(
    wl_hbm,
    wr_hbm,
    x_hbm,
    cs_hbm,
    ct_hbm,
    wq_hbm,
    wk_hbm,
    wv_hbm,
    wo_hbm,
    out_ref,
    x_ref,
    cs_ref,
    ct_ref,
    wqkv_ref,
    wo_ref,
    hsend,
    hrecv,
    active_ref,
    xcol,
    part_ref,
    settled_ref,
    moving_ref,
    stream_ref,
    normed_ref,
    packed_ref,
    blended_ref,
    back_ref,
    near_ref,
    q_ref,
    k_ref,
    v_ref,
    acc_ref,
    m_ref,
    l_ref,
    wl_ref,
    wr_ref,
    load_sem,
    hs_sem,
    hr_sem,
    ts_sem,
    tr_sem,
    gs_sem,
    gr_sem,
    zs_sem,
    zr_sem,
    bs_sem,
    br_sem,
):
    nt = lax.axis_size("tm")
    nh = lax.axis_size("height")
    it = lax.axis_index("tm")
    ih = lax.axis_index("height")
    t_next, t_prev = lax.rem(it + 1, nt), lax.rem(it + nt - 1, nt)
    h_next, h_prev = lax.rem(ih + 1, nh), lax.rem(ih + nh - 1, nh)

    team, mine, teams = it // F, lax.rem(it, F), nt // F

    loads = []
    for n, (src, dst) in enumerate(
        (
            (x_hbm, x_ref),
            (cs_hbm, cs_ref),
            (ct_hbm, ct_ref),
            (wq_hbm, wqkv_ref.at[pl.ds(0, C)]),
            (wk_hbm, wqkv_ref.at[pl.ds(C, C)]),
            (wv_hbm, wqkv_ref.at[pl.ds(2 * C, C)]),
            (wo_hbm, wo_ref),
            (wl_hbm, wl_ref),
            (wr_hbm, wr_ref),
        )
    ):
        copy = pltpu.make_async_copy(src, dst, load_sem.at[n])
        copy.start()
        loads.append(copy)

    barrier = pltpu.get_barrier_semaphore()
    friends = [(t_next, ih), (t_prev, ih), (it, h_next), (it, h_prev)]
    friends += [(F * team + lax.rem(mine + step, F), ih) for step in (1, 2, 3)]
    friends += [(lax.rem(it + F, nt), ih), (lax.rem(it + nt - F, nt), ih)]
    for dev in friends:
        pl.semaphore_signal(barrier, inc=1, device_id=dev, device_id_type=MESH)

    def remote(src, dst, ssem, rsem, dev):
        return pltpu.make_async_remote_copy(
            src_ref=src, dst_ref=dst, send_sem=ssem, recv_sem=rsem, device_id=dev, device_id_type=MESH
        )

    lane = lax.broadcasted_iota(jnp.int32, (C, LANES), 1)
    col = jnp.bitwise_and(lane, WIDE - 1)
    group = lax.shift_right_logical(lane, 5)

    loads[0].wait()
    top = jnp.zeros((C, LANES), F32)
    bottom = jnp.zeros((C, LANES), F32)
    for f in range(F):
        act = silu(x_ref[f].astype(F32))
        active_ref[f] = act
        top = jnp.where(group == f, roll(act, WIDE * f), top)
        bottom = jnp.where(group == f, roll(act, WIDE * f - 96), bottom)
    hsend[0] = bottom.astype(BF16)
    hsend[1] = top.astype(BF16)
    pl.semaphore_wait(barrier, len(friends))
    row_down = remote(hsend.at[0], hrecv.at[0], hs_sem.at[0], hr_sem.at[0], (it, h_next))
    row_up = remote(hsend.at[1], hrecv.at[1], hs_sem.at[1], hr_sem.at[1], (it, h_prev))
    row_down.start()
    row_up.start()

    def fill(n, k, a, rows):
        lanes = pl.ds(LANES * k, LANES)
        base = 3 * a * C
        xcol[n, pl.ds(base, C), lanes] = jnp.where(col == 0, 0.0, roll(rows, 1)).astype(BF16)
        xcol[n, pl.ds(base + C, C), lanes] = rows.astype(BF16)
        xcol[n, pl.ds(base + 2 * C, C), lanes] = jnp.where(col == WIDE - 1, 0.0, roll(rows, -1)).astype(BF16)

    for n in range(2):
        for k, f in enumerate(PAIRS[n]):
            fill(n, k, 1, active_ref[f])
    loads[1].wait()
    for n in range(2):
        part_ref[n] = jnp.dot(
            cs_ref[:, 1024:1920], xcol[n, pl.ds(1024, 896), :], preferred_element_type=F32
        )

    row_down.wait_recv()
    row_up.wait_recv()
    above = jnp.where(ih > 0, hrecv[0].astype(F32), 0.0)
    below = jnp.where(ih < nh - 1, hrecv[1].astype(F32), 0.0)

    def settle(n):
        for k, f in enumerate(PAIRS[n]):
            act = active_ref[f]
            fill(n, k, 0, jnp.where(group == 0, roll(above, -WIDE * f), roll(act, WIDE)))
            fill(n, k, 2, jnp.where(group == 3, roll(below, 96 - WIDE * f), roll(act, -WIDE)))
        total = part_ref[n]
        total += jnp.dot(cs_ref[:, 0:1024], xcol[n, pl.ds(0, 1024), :], preferred_element_type=F32)
        total += jnp.dot(cs_ref[:, 1920:2880], xcol[n, pl.ds(1920, 960), :], preferred_element_type=F32)
        for k, f in enumerate(PAIRS[n]):
            settled = (x_ref[f].astype(F32) + total[:, LANES * k : LANES * (k + 1)]).astype(BF16)
            settled_ref[f] = settled
            moving_ref[f + 1] = silu(settled.astype(F32)).astype(BF16)

    settle(0)
    to_next = remote(moving_ref.at[F], moving_ref.at[0], ts_sem.at[0], tr_sem.at[0], (t_next, ih))
    to_prev = remote(moving_ref.at[1], moving_ref.at[F + 1], ts_sem.at[1], tr_sem.at[1], (t_prev, ih))

    @pl.when(it < nt - 1)
    def _():
        to_next.start()

    @pl.when(it > 0)
    def _():
        to_prev.start()

    settle(1)

    def temporal(n):
        stacked = jnp.concatenate(
            [moving_ref[pl.ds(f, 3)].reshape(3 * C, LANES) for f in PAIRS[n]], axis=1
        )
        total = jnp.dot(ct_ref[...], stacked, preferred_element_type=F32)
        for k, f in enumerate(PAIRS[n]):
            stream = (settled_ref[f].astype(F32) + total[:, LANES * k : LANES * (k + 1)]).astype(BF16)
            stream_ref[f] = stream
            wide = stream.astype(F32)
            centred = wide - jnp.sum(wide, axis=0, keepdims=True) * (1.0 / C)
            spread = jnp.sum(centred * centred, axis=0, keepdims=True) * (1.0 / C)
            normed_ref[f] = centred * lax.rsqrt(spread + 1e-05)

    loads[2].wait()
    temporal(1)

    @pl.when(it > 0)
    def _():
        to_next.wait_recv()

    @pl.when(it < nt - 1)
    def _():
        to_prev.wait_recv()

    @pl.when(it == 0)
    def _():
        moving_ref[0] = jnp.zeros((C, LANES), BF16)

    @pl.when(it == nt - 1)
    def _():
        moving_ref[F + 1] = jnp.zeros((C, LANES), BF16)

    temporal(0)

    for j in range(F):
        row = jnp.zeros((C, LANES), F32)
        for f in range(F):
            row = jnp.where(group == f, roll(normed_ref[f], WIDE * (f - j)), row)
        packed_ref[j] = row.astype(BF16)

    def swap(step):
        other = lax.rem(mine + step, F)
        return remote(
            packed_ref.at[other],
            near_ref.at[2 + mine],
            gs_sem.at[step],
            gr_sem.at[mine],
            (F * team + other, ih),
        )

    def swapped(member):
        return remote(
            packed_ref.at[0], near_ref.at[2 + member], gs_sem.at[0], gr_sem.at[member], (it, h_next)
        )

    swaps = [swap(step) for step in (2, 1, 3)]
    for copy in swaps:
        copy.start()
    near_ref[2 + mine] = packed_ref[mine]

    def halo(member):
        late = member >= 2
        place = jnp.where(late, member - 2, member + 6)
        dev = (jnp.where(late, lax.rem(it + F, nt), lax.rem(it + nt - F, nt)), ih)
        return late, remote(
            near_ref.at[2 + member], near_ref.at[place], zs_sem.at[member], zr_sem.at[place], dev
        )

    def wanted(late):
        return jnp.where(late, jnp.where(team < teams - 1, 1, 0), jnp.where(team > 0, 1, 0)) == 1

    halos = []

    def send_halo(member):
        late, copy = halo(member)
        halos.append((late, copy))

        @pl.when(wanted(late))
        def _():
            copy.start()

    send_halo(mine)
    for n in (3, 4, 5, 7, 8):
        loads[n].wait()
    for step in (1, 3, 2):
        member = lax.rem(mine + step, F)
        swapped(member).wait_recv()
        send_halo(member)

    own = jnp.concatenate([near_ref[2 + i] for i in range(F)], axis=1)
    made = jnp.dot(wqkv_ref[...], own, preferred_element_type=F32)
    for i in range(F):
        part = made[:, LANES * i : LANES * (i + 1)]
        for r in range(F):
            q_ref[r, i] = roll(part[:C], WIDE * r).astype(BF16)
            v_ref[r, 2 + i] = roll(part[2 * C :], -WIDE * r).astype(BF16)
        k_ref[2 + i] = part[C : 2 * C].astype(BF16)

    def keys(first):
        near = jnp.concatenate([near_ref[first], near_ref[first + 1]], axis=1)
        made = jnp.dot(wqkv_ref[pl.ds(C, 2 * C)], near, preferred_element_type=F32)
        for i in range(2):
            part = made[:, LANES * i : LANES * (i + 1)]
            k_ref[first + i] = part[:C].astype(BF16)
            for r in range(F):
                v_ref[r, first + i] = roll(part[C:], -WIDE * r).astype(BF16)

    head_row = lax.broadcasted_iota(jnp.int32, (8, LANES), 0)
    lane_frame = lax.shift_right_logical(lax.broadcasted_iota(jnp.int32, (8, LANES), 1), 5)
    reach_left = jnp.zeros((8, LANES), jnp.int32)
    reach_right = jnp.zeros((8, LANES), jnp.int32)
    for h in range(HEADS):
        reach_left = jnp.where(head_row == h, wl_ref[h], reach_left)
        reach_right = jnp.where(head_row == h, wr_ref[h], reach_right)
    summing = jnp.where(
        lax.shift_right_logical(lax.broadcasted_iota(jnp.int32, (16, C), 1), 6)
        == lax.broadcasted_iota(jnp.int32, (16, C), 0),
        1.0,
        0.0,
    ).astype(BF16)

    def attend(i, blocks, fresh):
        masked = []
        for m in blocks:
            products = jnp.concatenate([q_ref[r, i] * k_ref[m] for r in range(F)], axis=1)
            scores = jnp.dot(summing, products, preferred_element_type=F32)[:8] * HEAD_DIM ** (-0.5)
            for r in range(F):
                turned = roll(scores[:, LANES * r : LANES * (r + 1)], -WIDE * r)
                offset = F * (m - 2 - i) + jnp.bitwise_and(lane_frame + r, F - 1) - lane_frame
                allowed = (offset >= -reach_left) & (offset <= reach_right)
                masked.append(jnp.where(allowed, turned, -1e30))
        highest = functools.reduce(jnp.maximum, masked)
        if not fresh:
            before = m_ref[i]
            highest = jnp.maximum(highest, before)
            fade = jnp.exp(before - highest)
        raised = [jnp.exp(one - highest) for one in masked]
        total = functools.reduce(jnp.add, raised)
        if not fresh:
            total = total + l_ref[i] * fade
        m_ref[i] = highest
        l_ref[i] = total
        for h in range(HEADS):
            rows = pl.ds(HEAD_DIM * h, HEAD_DIM)
            acc = None if fresh else acc_ref[i, rows] * fade[h : h + 1]
            for n, m in enumerate(blocks):
                for r in range(F):
                    term = raised[F * n + r][h : h + 1] * v_ref[r, m, rows].astype(F32)
                    acc = term if acc is None else acc + term
            acc_ref[i, rows] = acc

    def loop(low, high, blocks, fresh):
        def step(i, carry):
            attend(i, blocks, fresh)
            return carry

        lax.fori_loop(low, high, step, 0)

    def finish(i):
        scale = 1.0 / l_ref[i]
        blended_ref[i] = jnp.concatenate(
            [
                (acc_ref[i, pl.ds(HEAD_DIM * h, HEAD_DIM)] * scale[h : h + 1]).astype(BF16)
                for h in range(HEADS)
            ],
            axis=0,
        )
        copy = remote(
            blended_ref.at[i], back_ref.at[mine], bs_sem.at[i], br_sem.at[mine], (F * team + i, ih)
        )

        @pl.when(mine != i)
        def _():
            copy.start()

        @pl.when(mine == i)
        def _():
            back_ref[mine] = blended_ref[i]

        return copy

    loop(0, F, (2, 3, 4, 5), True)

    def received(place):
        remote(near_ref.at[2], near_ref.at[place], zs_sem.at[0], zr_sem.at[place], (it, h_next)).wait_recv()

    @pl.when(team > 0)
    def _():
        received(0)
        received(1)
        keys(0)
        loop(0, 2, (0, 1), False)

    backs = [finish(0), finish(1)]

    @pl.when(team < teams - 1)
    def _():
        received(6)
        received(7)
        keys(6)
        loop(2, 4, (6, 7), False)

    backs += [finish(2), finish(3)]

    loads[6].wait()
    for step in (1, 3, 2):
        member = lax.rem(mine + step, F)
        remote(
            blended_ref.at[0], back_ref.at[member], bs_sem.at[0], br_sem.at[member], (it, h_next)
        ).wait_recv()
    mixed = jnp.dot(
        wo_ref[...],
        jnp.concatenate([back_ref[j] for j in range(F)], axis=1),
        preferred_element_type=F32,
    )
    for f in range(F):
        whole = jnp.zeros((C, LANES), F32)
        for j in range(F):
            whole = jnp.where(group == j, roll(mixed[:, LANES * j : LANES * (j + 1)], WIDE * (j - f)), whole)
        out_ref[f] = (stream_ref[f].astype(F32) + whole).astype(BF16)

    row_down.wait_send()
    row_up.wait_send()

    @pl.when(it < nt - 1)
    def _():
        to_next.wait_send()

    @pl.when(it > 0)
    def _():
        to_prev.wait_send()

    for copy in swaps:
        copy.wait_send()
    for late, copy in halos:

        @pl.when(wanted(late))
        def _():
            copy.wait_send()

    for i in range(F):

        @pl.when(mine != i)
        def _():
            backs[i].wait_send()


def per_device(
    frames_in, conv_spatial, conv_temporal, w_query, w_key, w_value, w_out, win_left, win_right
):
    hbm = pl.BlockSpec(memory_space=pltpu.HBM)
    frame = (C, LANES)
    return pl.pallas_call(
        kernel,
        out_shape=jax.ShapeDtypeStruct(frames_in.shape, BF16),
        in_specs=[hbm] * 9,
        out_specs=pl.BlockSpec(memory_space=pltpu.VMEM),
        scratch_shapes=[
            pltpu.VMEM((F,) + frame, BF16),
            pltpu.VMEM((C, 9 * C), BF16),
            pltpu.VMEM((C, 3 * C), BF16),
            pltpu.VMEM((3 * C, C), BF16),
            pltpu.VMEM((C, C), BF16),
            pltpu.VMEM((2,) + frame, BF16),
            pltpu.VMEM((2,) + frame, BF16),
            pltpu.VMEM((F,) + frame, F32),
            pltpu.VMEM((2, 9 * C, 2 * LANES), BF16),
            pltpu.VMEM((2, C, 2 * LANES), F32),
            pltpu.VMEM((F,) + frame, BF16),
            pltpu.VMEM((F + 2,) + frame, BF16),
            pltpu.VMEM((F,) + frame, BF16),
            pltpu.VMEM((F,) + frame, F32),
            pltpu.VMEM((F,) + frame, BF16),
            pltpu.VMEM((F,) + frame, BF16),
            pltpu.VMEM((F,) + frame, BF16),
            pltpu.VMEM((2 * F,) + frame, BF16),
            pltpu.VMEM((F, F) + frame, BF16),
            pltpu.VMEM((2 * F,) + frame, BF16),
            pltpu.VMEM((F, 2 * F) + frame, BF16),
            pltpu.VMEM((F,) + frame, F32),
            pltpu.VMEM((F, 8, LANES), F32),
            pltpu.VMEM((F, 8, LANES), F32),
            pltpu.SMEM((HEADS,), jnp.int32),
            pltpu.SMEM((HEADS,), jnp.int32),
            pltpu.SemaphoreType.DMA((9,)),
            pltpu.SemaphoreType.DMA((2,)),
            pltpu.SemaphoreType.DMA((2,)),
            pltpu.SemaphoreType.DMA((2,)),
            pltpu.SemaphoreType.DMA((2,)),
            pltpu.SemaphoreType.DMA((F,)),
            pltpu.SemaphoreType.DMA((F,)),
            pltpu.SemaphoreType.DMA((F,)),
            pltpu.SemaphoreType.DMA((2 * F,)),
            pltpu.SemaphoreType.DMA((F,)),
            pltpu.SemaphoreType.DMA((F,)),
        ],
        compiler_params=pltpu.CompilerParams(
            collective_id=0, has_side_effects=True, vmem_limit_bytes=62 * 1024 * 1024
        ),
    )(win_left, win_right, frames_in, conv_spatial, conv_temporal, w_query, w_key, w_value, w_out)


def solution(mesh):
    return jax.shard_map(
        per_device,
        mesh=mesh,
        in_specs=(P("tm", None, "height"), P(), P(), P(), P(), P(), P(), P(), P()),
        out_specs=P("tm", None, "height"),
        check_vma=False,
    )
```

time: 58.2 us -> 45 us (0.77)
  the two profiles are of different devices: /device:TPU:1 before, /device:TPU:22 now
where the time goes in v2:
time: 45 us; the launch traced here: 44.9 us
  Pallas kernels  43.1 us (96%)
  local copies, waits for them, and re-layouts  1.72 us (4%)
    pallas_call x1, Pallas kernels, per_device(): pl.pallas_call(kernel, out_shape=jax.ShapeDtypeStruct(frames_in.shape, BF...  43.1 us
    unnamed x1, local copies, waits for them, and re-layouts  1.72 us

profile of v2, /device:TPU:22, one launch (start us, length us, event | category | flops | bytes accessed | tf_op | source)
XLA Modules:
  0.0 44.9 jit_solution(5658715019147836854)
XLA Ops:
  0.0 43.1 %shard_map.91 = bf16[4,320,128]{2,1,0:T(8,128)(2,1)} custom-call(s32[5]{0:T(128)} %wl_hbm.1, s32[5]{0:T(128)} %wr_hbm.1, bf16[4,320,128]{2,1,0:T(8,128)(2,1)} %x_hbm.1, bf16[320,2880]{1,0:T(8,128)(2,1)} %cs_hbm.1, bf16[320,960]{1,0:T(8,128)(2,1)} %ct_hbm.1, bf16[320,320]{1,0:T(8,128)(2,1)} %wq_hbm.1, bf16[320,320]{1,0:T(8,128)(2,1)} %wk_hbm.1, ...), custom_call_target="tpu_custom_call" | custom-call | tf_op jit(solution)/shard_map/pallas_call | solution.py:439
  43.2 1.7 %copy.11 = bf16[4,320,128]{2,1,0:T(8,128)(2,1)} copy(bf16[4,320,128]{2,1,0:T(8,128)(2,1)} %shard_map.91) | data formatting | bytes 655360

commit v3 on v2

v3 whole, which is shorter than its diff:
```python
import functools

import jax
import jax.numpy as jnp
from jax import lax
from jax.experimental import pallas as pl
from jax.experimental.pallas import tpu as pltpu
from jax.sharding import PartitionSpec as P

HEADS = 5
HEAD_DIM = 64
WIDE = 32
C = 320
F = 4
LANES = 128
QUARTER = C // F
MESH = pl.DeviceIdType.MESH
F32 = jnp.float32
BF16 = jnp.bfloat16


def silu(v):
    return 0.5 * v * (1.0 + jnp.tanh(0.5 * v))


def roll(v, shift):
    shift = shift % LANES
    return v if shift == 0 else pltpu.roll(v, shift, 1)


def kernel(
    wl_hbm,
    wr_hbm,
    x_hbm,
    cs_hbm,
    ct_hbm,
    wq_hbm,
    wk_hbm,
    wv_hbm,
    wo_hbm,
    out_ref,
    x_ref,
    cs_ref,
    ct_ref,
    wqkv_ref,
    wo_ref,
    wl_ref,
    wr_ref,
    rows_ref,
    taps_ref,
    above_ref,
    settled_ref,
    edge_ref,
    near_ref,
    far_ref,
    steps_ref,
    stream_ref,
    done_ref,
    back_ref,
    q_ref,
    k_ref,
    v_ref,
    acc_ref,
    m_ref,
    l_ref,
    load_sem,
    hs_sem,
    hr_sem,
    gs_sem,
    gr_sem,
    es_sem,
    er_sem,
    zs_sem,
    zr_sem,
    bs_sem,
    br_sem,
):
    nt = lax.axis_size("tm")
    nh = lax.axis_size("height")
    it = lax.axis_index("tm")
    ih = lax.axis_index("height")
    h_next, h_prev = lax.rem(ih + 1, nh), lax.rem(ih + nh - 1, nh)
    team, mine, teams = it // F, lax.rem(it, F), nt // F
    odd = lax.rem(mine, 2)
    later, earlier = lax.rem(team + 1, teams), lax.rem(team + teams - 1, teams)

    loads = []
    for n, (src, dst) in enumerate(
        (
            (x_hbm, x_ref),
            (cs_hbm, cs_ref),
            (ct_hbm, ct_ref),
            (wq_hbm, wqkv_ref.at[pl.ds(0, C)]),
            (wk_hbm, wqkv_ref.at[pl.ds(C, C)]),
            (wv_hbm, wqkv_ref.at[pl.ds(2 * C, C)]),
            (wo_hbm, wo_ref),
            (wl_hbm, wl_ref),
            (wr_hbm, wr_ref),
        )
    ):
        copy = pltpu.make_async_copy(src, dst, load_sem.at[n])
        copy.start()
        loads.append(copy)

    barrier = pltpu.get_barrier_semaphore()
    friends = [(it, h_next), (it, h_prev)]
    friends += [(F * team + lax.rem(mine + step, F), ih) for step in (1, 2, 3)]
    friends += [(F * later + mine, ih), (F * earlier + mine, ih)]
    friends += [(F * earlier + 1, ih), (F * earlier + 3, ih), (F * later, ih), (F * later + 2, ih)]
    for dev in friends:
        pl.semaphore_signal(barrier, inc=1, device_id=dev, device_id_type=MESH)

    def remote(src, dst, ssem, rsem, dev):
        return pltpu.make_async_remote_copy(
            src_ref=src, dst_ref=dst, send_sem=ssem, recv_sem=rsem, device_id=dev, device_id_type=MESH
        )

    lane = lax.broadcasted_iota(jnp.int32, (C, LANES), 1)
    col = jnp.bitwise_and(lane, WIDE - 1)
    group = lax.shift_right_logical(lane, 5)
    block_group = lax.shift_right_logical(lax.broadcasted_iota(jnp.int32, (QUARTER, LANES), 1), 5)

    def fill(place, act):
        taps_ref[place, pl.ds(0, C)] = jnp.where(col == 0, 0.0, roll(act, 1)).astype(BF16)
        taps_ref[place, pl.ds(C, C)] = act.astype(BF16)
        taps_ref[place, pl.ds(2 * C, C)] = jnp.where(col == WIDE - 1, 0.0, roll(act, -1)).astype(BF16)

    loads[0].wait()
    frames = [x_ref[f].astype(F32) for f in range(F)]
    for j in range(F):
        row = jnp.zeros((C, LANES), F32)
        for f in range(F):
            row = jnp.where(group == f, roll(frames[f], WIDE * (f - j)), row)
        rows_ref[j] = row
        fill(j + 1, silu(row))

    pl.semaphore_wait(barrier, len(friends))
    row_down = remote(
        taps_ref.at[F, pl.ds(C, C)], above_ref.at[0], hs_sem.at[0], hr_sem.at[0], (it, h_next)
    )
    row_up = remote(
        taps_ref.at[1, pl.ds(C, C)], above_ref.at[1], hs_sem.at[1], hr_sem.at[1], (it, h_prev)
    )
    row_down.start()
    row_up.start()

    def around(j):
        return taps_ref[pl.ds(j, 3)].reshape(9 * C, LANES)

    def product(weights, source):
        return jnp.dot(weights, source, preferred_element_type=F32)

    swaps, edges = {}, {}
    edge_team = jnp.where(odd == 1, later, earlier)
    edge_slot = jnp.where(odd == 1, 0, 2) + mine // 2
    edge_wanted = jnp.where(odd == 1, jnp.where(team < teams - 1, 1, 0), jnp.where(team > 0, 1, 0)) == 1

    def settle(j, spatial):
        settled = (rows_ref[j] + spatial).astype(BF16)
        settled_ref[j] = settled
        wide = settled.astype(F32)
        swaps[j] = remote(
            settled_ref.at[j], near_ref.at[2 + mine], gs_sem.at[j], gr_sem.at[mine], (F * team + j, ih)
        )

        @pl.when(mine != j)
        def _():
            swaps[j].start()

        @pl.when(mine == j)
        def _():
            near_ref[2 + j] = settled

        block = jnp.zeros((QUARTER, LANES), F32)
        for n in range(F):
            part = wide[QUARTER * n : QUARTER * (n + 1)]
            turned = jnp.where(odd == 1, roll(part, WIDE * (n + 1)), roll(part, WIDE * n))
            block = jnp.where(block_group == n, turned, block)
        edge_ref[j] = block.astype(BF16)
        edges[j] = remote(
            edge_ref.at[j], far_ref.at[edge_slot], es_sem.at[j], er_sem.at[edge_slot], (F * edge_team + j, ih)
        )

        @pl.when(edge_wanted)
        def _():
            edges[j].start()

    loads[1].wait()
    inner = product(cs_ref[...], jnp.concatenate([around(1), around(2)], axis=1))
    settle(1, inner[:, :LANES])
    settle(2, inner[:, LANES:])
    upper = product(cs_ref[:, 1024:2880], around(0)[1024:2880])
    lower = product(cs_ref[:, 0:1920], around(3)[0:1920])

    row_down.wait_recv()
    row_up.wait_recv()
    fill(0, jnp.where(ih > 0, above_ref[0].astype(F32), 0.0))
    fill(F + 1, jnp.where(ih < nh - 1, above_ref[1].astype(F32), 0.0))
    settle(0, upper + product(cs_ref[:, 0:1024], around(0)[0:1024]))
    settle(3, lower + product(cs_ref[:, 1920:2880], around(3)[1920:2880]))

    def swapped(member):
        return remote(
            settled_ref.at[0], near_ref.at[2 + member], gs_sem.at[0], gr_sem.at[member], (it, h_next)
        )

    def wanted(late):
        return jnp.where(late, jnp.where(team < teams - 1, 1, 0), jnp.where(team > 0, 1, 0)) == 1

    halos = []

    def send_halo(member):
        late = member >= 2
        place = jnp.where(late, member - 2, member + 6)
        copy = remote(
            near_ref.at[2 + member],
            near_ref.at[place],
            zs_sem.at[member],
            zr_sem.at[place],
            (F * jnp.where(late, later, earlier) + mine, ih),
        )
        halos.append((late, copy))

        @pl.when(wanted(late))
        def _():
            copy.start()

    send_halo(mine)
    for n in (2, 3, 4, 5, 6, 7, 8):
        loads[n].wait()
    for step in (1, 3, 2):
        member = lax.rem(mine + step, F)
        swapped(member).wait_recv()
        send_halo(member)

    def edge_arrived(slot):
        remote(edge_ref.at[0], far_ref.at[slot], es_sem.at[0], er_sem.at[slot], (it, h_next)).wait_recv()

    def halo_arrived(place):
        remote(near_ref.at[2], near_ref.at[place], zs_sem.at[0], zr_sem.at[place], (it, h_next)).wait_recv()

    @pl.when(team > 0)
    def _():
        edge_arrived(1)

    @pl.when(team < teams - 1)
    def _():
        edge_arrived(2)

    def edge_frame(slot, there, place):
        block = silu(jnp.where(there, far_ref[slot].astype(F32), 0.0))
        return jnp.concatenate([roll(block, WIDE * (place - n)) for n in range(F)], axis=0)

    def temporal(first, count, before, after):
        ahead, behind = [], []
        for m in range(count):
            moving = silu(near_ref[first + m].astype(F32))
            steps_ref[m, pl.ds(C, C)] = moving.astype(BF16)
            ahead.append(roll(moving, WIDE))
            behind.append(roll(moving, -WIDE))
        for m in range(count):
            left = before if m == 0 else ahead[m - 1]
            right = after if m == count - 1 else behind[m + 1]
            steps_ref[m, pl.ds(0, C)] = jnp.where(group == 0, left, ahead[m]).astype(BF16)
            steps_ref[m, pl.ds(2 * C, C)] = jnp.where(group == F - 1, right, behind[m]).astype(BF16)
        total = product(ct_ref[...], jnp.concatenate([steps_ref[m] for m in range(count)], axis=1))
        streams, normed = [], []
        for m in range(count):
            stream = (near_ref[first + m].astype(F32) + total[:, LANES * m : LANES * (m + 1)]).astype(BF16)
            wide = stream.astype(F32)
            centred = wide - jnp.sum(wide, axis=0, keepdims=True) * (1.0 / C)
            spread = jnp.sum(centred * centred, axis=0, keepdims=True) * (1.0 / C)
            streams.append(stream)
            normed.append((centred * lax.rsqrt(spread + 1e-05)).astype(BF16))
        return streams, jnp.concatenate(normed, axis=1)

    streams, normed = temporal(2, F, edge_frame(1, team > 0, 0), edge_frame(2, team < teams - 1, F - 1))
    made = product(wqkv_ref[...], normed)
    for i in range(F):
        stream_ref[i] = streams[i]
        part = made[:, LANES * i : LANES * (i + 1)]
        for r in range(F):
            q_ref[r, i] = roll(part[:C], WIDE * r).astype(BF16)
            v_ref[r, 2 + i] = roll(part[2 * C :], -WIDE * r).astype(BF16)
        k_ref[2 + i] = part[C : 2 * C].astype(BF16)

    def keys(first, normed):
        made = product(wqkv_ref[pl.ds(C, 2 * C)], normed)
        for i in range(2):
            part = made[:, LANES * i : LANES * (i + 1)]
            k_ref[first + i] = part[:C].astype(BF16)
            for r in range(F):
                v_ref[r, first + i] = roll(part[C:], -WIDE * r).astype(BF16)

    head_row = lax.broadcasted_iota(jnp.int32, (8, LANES), 0)
    lane_frame = lax.shift_right_logical(lax.broadcasted_iota(jnp.int32, (8, LANES), 1), 5)
    reach_left = jnp.zeros((8, LANES), jnp.int32)
    reach_right = jnp.zeros((8, LANES), jnp.int32)
    for h in range(HEADS):
        reach_left = jnp.where(head_row == h, wl_ref[h], reach_left)
        reach_right = jnp.where(head_row == h, wr_ref[h], reach_right)
    summing = jnp.where(
        lax.shift_right_logical(lax.broadcasted_iota(jnp.int32, (16, C), 1), 6)
        == lax.broadcasted_iota(jnp.int32, (16, C), 0),
        1.0,
        0.0,
    ).astype(BF16)

    def attend(i, blocks, fresh):
        masked = []
        for m in blocks:
            products = jnp.concatenate([q_ref[r, i] * k_ref[m] for r in range(F)], axis=1)
            scores = product(summing, products)[:8] * HEAD_DIM ** (-0.5)
            for r in range(F):
                turned = roll(scores[:, LANES * r : LANES * (r + 1)], -WIDE * r)
                offset = F * (m - 2 - i) + jnp.bitwise_and(lane_frame + r, F - 1) - lane_frame
                allowed = (offset >= -reach_left) & (offset <= reach_right)
                masked.append(jnp.where(allowed, turned, -1e30))
        highest = functools.reduce(jnp.maximum, masked)
        if not fresh:
            before = m_ref[i]
            highest = jnp.maximum(highest, before)
            fade = jnp.exp(before - highest)
        raised = [jnp.exp(one - highest) for one in masked]
        total = functools.reduce(jnp.add, raised)
        if not fresh:
            total = total + l_ref[i] * fade
        m_ref[i] = highest
        l_ref[i] = total
        for h in range(HEADS):
            rows = pl.ds(HEAD_DIM * h, HEAD_DIM)
            acc = None if fresh else acc_ref[i, rows] * fade[h : h + 1]
            for n, m in enumerate(blocks):
                for r in range(F):
                    term = raised[F * n + r][h : h + 1] * v_ref[r, m, rows].astype(F32)
                    acc = term if acc is None else acc + term
            acc_ref[i, rows] = acc

    def loop(low, high, blocks, fresh):
        def step(i, carry):
            attend(i, blocks, fresh)
            return carry

        lax.fori_loop(low, high, step, 0)

    backs = {}

    def finish(pair):
        blended = []
        for i in pair:
            scale = 1.0 / l_ref[i]
            blended.append(
                jnp.concatenate(
                    [
                        (acc_ref[i, pl.ds(HEAD_DIM * h, HEAD_DIM)] * scale[h : h + 1]).astype(BF16)
                        for h in range(HEADS)
                    ],
                    axis=0,
                )
            )
        mixed = product(wo_ref[...], jnp.concatenate(blended, axis=1))
        for n, i in enumerate(pair):
            done = (stream_ref[i].astype(F32) + mixed[:, LANES * n : LANES * (n + 1)]).astype(BF16)
            done_ref[i] = done
            backs[i] = remote(
                done_ref.at[i], back_ref.at[mine], bs_sem.at[i], br_sem.at[mine], (F * team + i, ih)
            )

            @pl.when(mine != i)
            def _():
                backs[i].start()

            @pl.when(mine == i)
            def _():
                back_ref[mine] = done

    loop(0, F, (2, 3, 4, 5), True)

    @pl.when(team < teams - 1)
    def _():
        edge_arrived(3)
        halo_arrived(6)
        halo_arrived(7)
        before = roll(silu(near_ref[5].astype(F32)), WIDE)
        keys(6, temporal(6, 2, before, edge_frame(3, True, F - 1))[1])
        loop(2, 4, (6, 7), False)

    finish((2, 3))

    @pl.when(team > 0)
    def _():
        edge_arrived(0)
        halo_arrived(0)
        halo_arrived(1)
        after = roll(silu(near_ref[2].astype(F32)), -WIDE)
        keys(0, temporal(0, 2, edge_frame(0, True, 0), after)[1])
        loop(0, 2, (0, 1), False)

    finish((0, 1))

    for step in (1, 3, 2):
        member = lax.rem(mine + step, F)
        remote(
            done_ref.at[0], back_ref.at[member], bs_sem.at[0], br_sem.at[member], (it, h_next)
        ).wait_recv()
    lines = [back_ref[j].astype(F32) for j in range(F)]
    for f in range(F):
        whole = lines[0] if f == 0 else roll(lines[0], -WIDE * f)
        for j in range(1, F):
            whole = jnp.where(group == j, roll(lines[j], WIDE * (j - f)), whole)
        out_ref[f] = whole.astype(BF16)

    row_down.wait_send()
    row_up.wait_send()
    for j in range(F):

        @pl.when(mine != j)
        def _():
            swaps[j].wait_send()
            backs[j].wait_send()

        @pl.when(edge_wanted)
        def _():
            edges[j].wait_send()

    for late, copy in halos:

        @pl.when(wanted(late))
        def _():
            copy.wait_send()


def per_device(
    frames_in, conv_spatial, conv_temporal, w_query, w_key, w_value, w_out, win_left, win_right
):
    hbm = pl.BlockSpec(memory_space=pltpu.HBM)
    frame = (C, LANES)
    return pl.pallas_call(
        kernel,
        out_shape=jax.ShapeDtypeStruct(frames_in.shape, BF16),
        in_specs=[hbm] * 9,
        out_specs=pl.BlockSpec(memory_space=pltpu.VMEM),
        scratch_shapes=[
            pltpu.VMEM((F,) + frame, BF16),
            pltpu.VMEM((C, 9 * C), BF16),
            pltpu.VMEM((C, 3 * C), BF16),
            pltpu.VMEM((3 * C, C), BF16),
            pltpu.VMEM((C, C), BF16),
            pltpu.SMEM((HEADS,), jnp.int32),
            pltpu.SMEM((HEADS,), jnp.int32),
            pltpu.VMEM((F,) + frame, F32),
            pltpu.VMEM((F + 2, 3 * C, LANES), BF16),
            pltpu.VMEM((2,) + frame, BF16),
            pltpu.VMEM((F,) + frame, BF16),
            pltpu.VMEM((F, QUARTER, LANES), BF16),
            pltpu.VMEM((2 * F,) + frame, BF16),
            pltpu.VMEM((F, QUARTER, LANES), BF16),
            pltpu.VMEM((F, 3 * C, LANES), BF16),
            pltpu.VMEM((F,) + frame, BF16),
            pltpu.VMEM((F,) + frame, BF16),
            pltpu.VMEM((F,) + frame, BF16),
            pltpu.VMEM((F, F) + frame, BF16),
            pltpu.VMEM((2 * F,) + frame, BF16),
            pltpu.VMEM((F, 2 * F) + frame, BF16),
            pltpu.VMEM((F,) + frame, F32),
            pltpu.VMEM((F, 8, LANES), F32),
            pltpu.VMEM((F, 8, LANES), F32),
            pltpu.SemaphoreType.DMA((9,)),
            pltpu.SemaphoreType.DMA((2,)),
            pltpu.SemaphoreType.DMA((2,)),
            pltpu.SemaphoreType.DMA((F,)),
            pltpu.SemaphoreType.DMA((F,)),
            pltpu.SemaphoreType.DMA((F,)),
            pltpu.SemaphoreType.DMA((F,)),
            pltpu.SemaphoreType.DMA((F,)),
            pltpu.SemaphoreType.DMA((2 * F,)),
            pltpu.SemaphoreType.DMA((F,)),
            pltpu.SemaphoreType.DMA((F,)),
        ],
        compiler_params=pltpu.CompilerParams(
            collective_id=0, has_side_effects=True, vmem_limit_bytes=62 * 1024 * 1024
        ),
    )(win_left, win_right, frames_in, conv_spatial, conv_temporal, w_query, w_key, w_value, w_out)


def solution(mesh):
    return jax.shard_map(
        per_device,
        mesh=mesh,
        in_specs=(P("tm", None, "height"), P(), P(), P(), P(), P(), P(), P(), P()),
        out_specs=P("tm", None, "height"),
        check_vma=False,
    )
```

time: 45 us -> 41.6 us (0.924)
  the two profiles are of different devices: /device:TPU:22 before, /device:TPU:2 now
where the time goes in v3:
time: 41.6 us; the launch traced here: 41.5 us
  Pallas kernels  39.7 us (95%)
  local copies, waits for them, and re-layouts  1.72 us (4%)
    pallas_call x1, Pallas kernels, per_device(): pl.pallas_call(kernel, out_shape=jax.ShapeDtypeStruct(frames_in.shape, BF...  39.7 us
    unnamed x1, local copies, waits for them, and re-layouts  1.72 us

profile of v3, /device:TPU:2, one launch (start us, length us, event | category | flops | bytes accessed | tf_op | source)
XLA Modules:
  0.0 41.5 jit_solution(5339379010211339708)
XLA Ops:
  0.0 39.7 %shard_map.91 = bf16[4,320,128]{2,1,0:T(8,128)(2,1)} custom-call(s32[5]{0:T(128)} %wl_hbm.1, s32[5]{0:T(128)} %wr_hbm.1, bf16[4,320,128]{2,1,0:T(8,128)(2,1)} %x_hbm.1, bf16[320,2880]{1,0:T(8,128)(2,1)} %cs_hbm.1, bf16[320,960]{1,0:T(8,128)(2,1)} %ct_hbm.1, bf16[320,320]{1,0:T(8,128)(2,1)} %wq_hbm.1, bf16[320,320]{1,0:T(8,128)(2,1)} %wk_hbm.1, ...), custom_call_target="tpu_custom_call" | custom-call | tf_op jit(solution)/shard_map/pallas_call | solution.py:438
  39.7 1.7 %copy.11 = bf16[4,320,128]{2,1,0:T(8,128)(2,1)} copy(bf16[4,320,128]{2,1,0:T(8,128)(2,1)} %shard_map.91) | data formatting | bytes 655360

commit v4 on v3

--- a/solution.py
+++ b/solution.py
@@ -57,6 +57,7 @@
     stream_ref,
     done_ref,
     back_ref,
+    rim_ref,
     q_ref,
     k_ref,
     v_ref,
@@ -105,10 +106,21 @@
     barrier = pltpu.get_barrier_semaphore()
     friends = [(it, h_next), (it, h_prev)]
     friends += [(F * team + lax.rem(mine + step, F), ih) for step in (1, 2, 3)]
-    friends += [(F * later + mine, ih), (F * earlier + mine, ih)]
-    friends += [(F * earlier + 1, ih), (F * earlier + 3, ih), (F * later, ih), (F * later + 2, ih)]
     for dev in friends:
         pl.semaphore_signal(barrier, inc=1, device_id=dev, device_id_type=MESH)
+
+    @pl.when(team > 0)
+    def _():
+        for dev in ((F * earlier + mine, ih), (F * earlier + 1, ih), (F * earlier + 3, ih)):
+            pl.semaphore_signal(barrier, inc=1, device_id=dev, device_id_type=MESH)
+
+    @pl.when(team < teams - 1)
+    def _():
+        for dev in ((F * later + mine, ih), (F * later, ih), (F * later + 2, ih)):
+            pl.semaphore_signal(barrier, inc=1, device_id=dev, device_id_type=MESH)
+
+    has_later, has_earlier = jnp.where(team < teams - 1, 1, 0), jnp.where(team > 0, 1, 0)
+    greetings = len(friends) + has_later * (1 + F * odd) + has_earlier * (1 + F * (1 - odd))
 
     def remote(src, dst, ssem, rsem, dev):
         return pltpu.make_async_remote_copy(
@@ -134,7 +146,7 @@
         rows_ref[j] = row
         fill(j + 1, silu(row))
 
-    pl.semaphore_wait(barrier, len(friends))
+    pl.semaphore_wait(barrier, greetings)
     row_down = remote(
         taps_ref.at[F, pl.ds(C, C)], above_ref.at[0], hs_sem.at[0], hr_sem.at[0], (it, h_next)
     )
@@ -189,15 +201,13 @@
     inner = product(cs_ref[...], jnp.concatenate([around(1), around(2)], axis=1))
     settle(1, inner[:, :LANES])
     settle(2, inner[:, LANES:])
-    upper = product(cs_ref[:, 1024:2880], around(0)[1024:2880])
-    lower = product(cs_ref[:, 0:1920], around(3)[0:1920])
-
     row_down.wait_recv()
     row_up.wait_recv()
     fill(0, jnp.where(ih > 0, above_ref[0].astype(F32), 0.0))
     fill(F + 1, jnp.where(ih < nh - 1, above_ref[1].astype(F32), 0.0))
-    settle(0, upper + product(cs_ref[:, 0:1024], around(0)[0:1024]))
-    settle(3, lower + product(cs_ref[:, 1920:2880], around(3)[1920:2880]))
+    outer = product(cs_ref[...], jnp.concatenate([around(0), around(3)], axis=1))
+    settle(0, outer[:, :LANES])
+    settle(3, outer[:, LANES:])
 
     def swapped(member):
         return remote(
@@ -251,46 +261,45 @@
         block = silu(jnp.where(there, far_ref[slot].astype(F32), 0.0))
         return jnp.concatenate([roll(block, WIDE * (place - n)) for n in range(F)], axis=0)
 
-    def temporal(first, count, before, after):
+    def temporal(values, lefts, rights):
         ahead, behind = [], []
-        for m in range(count):
-            moving = silu(near_ref[first + m].astype(F32))
+        for m in range(F):
+            moving = silu(values[m])
             steps_ref[m, pl.ds(C, C)] = moving.astype(BF16)
             ahead.append(roll(moving, WIDE))
             behind.append(roll(moving, -WIDE))
-        for m in range(count):
-            left = before if m == 0 else ahead[m - 1]
-            right = after if m == count - 1 else behind[m + 1]
+        for m in range(F):
+            left = ahead[m - 1] if lefts[m] is None else lefts[m]
+            right = behind[m + 1] if rights[m] is None else rights[m]
             steps_ref[m, pl.ds(0, C)] = jnp.where(group == 0, left, ahead[m]).astype(BF16)
             steps_ref[m, pl.ds(2 * C, C)] = jnp.where(group == F - 1, right, behind[m]).astype(BF16)
-        total = product(ct_ref[...], jnp.concatenate([steps_ref[m] for m in range(count)], axis=1))
+        total = product(ct_ref[...], jnp.concatenate([steps_ref[m] for m in range(F)], axis=1))
         streams, normed = [], []
-        for m in range(count):
-            stream = (near_ref[first + m].astype(F32) + total[:, LANES * m : LANES * (m + 1)]).astype(BF16)
+        for m in range(F):
+            stream = (values[m] + total[:, LANES * m : LANES * (m + 1)]).astype(BF16)
             wide = stream.astype(F32)
             centred = wide - jnp.sum(wide, axis=0, keepdims=True) * (1.0 / C)
             spread = jnp.sum(centred * centred, axis=0, keepdims=True) * (1.0 / C)
             streams.append(stream)
             normed.append((centred * lax.rsqrt(spread + 1e-05)).astype(BF16))
-        return streams, jnp.concatenate(normed, axis=1)
-
-    streams, normed = temporal(2, F, edge_frame(1, team > 0, 0), edge_frame(2, team < teams - 1, F - 1))
+        return streams, jnp.concatenate(normed, axis=1), behind[0], ahead[F - 1]
+
+    streams, normed, first_frame, last_frame = temporal(
+        [near_ref[2 + i].astype(F32) for i in range(F)],
+        [edge_frame(1, team > 0, 0), None, None, None],
+        [None, None, None, edge_frame(2, team < teams - 1, F - 1)],
+    )
+    rim_ref[0] = first_frame
+    rim_ref[1] = last_frame
     made = product(wqkv_ref[...], normed)
     for i in range(F):
         stream_ref[i] = streams[i]
         part = made[:, LANES * i : LANES * (i + 1)]
+        query, value = part[:C].astype(BF16), part[2 * C :].astype(BF16)
         for r in range(F):
-            q_ref[r, i] = roll(part[:C], WIDE * r).astype(BF16)
-            v_ref[r, 2 + i] = roll(part[2 * C :], -WIDE * r).astype(BF16)
+            q_ref[r, i] = roll(query, WIDE * r)
+            v_ref[r, 2 + i] = roll(value, -WIDE * r)
         k_ref[2 + i] = part[C : 2 * C].astype(BF16)
-
-    def keys(first, normed):
-        made = product(wqkv_ref[pl.ds(C, 2 * C)], normed)
-        for i in range(2):
-            part = made[:, LANES * i : LANES * (i + 1)]
-            k_ref[first + i] = part[:C].astype(BF16)
-            for r in range(F):
-                v_ref[r, first + i] = roll(part[C:], -WIDE * r).astype(BF16)
 
     head_row = lax.broadcasted_iota(jnp.int32, (8, LANES), 0)
     lane_frame = lax.shift_right_logical(lax.broadcasted_iota(jnp.int32, (8, LANES), 1), 5)
@@ -306,7 +315,7 @@
         0.0,
     ).astype(BF16)
 
-    def attend(i, blocks, fresh):
+    def attend(i, blocks, fresh, known=None):
         masked = []
         for m in blocks:
             products = jnp.concatenate([q_ref[r, i] * k_ref[m] for r in range(F)], axis=1)
@@ -314,6 +323,8 @@
             for r in range(F):
                 turned = roll(scores[:, LANES * r : LANES * (r + 1)], -WIDE * r)
                 offset = F * (m - 2 - i) + jnp.bitwise_and(lane_frame + r, F - 1) - lane_frame
+                if known is not None:
+                    offset = jnp.where(known, offset, 2 * LANES)
                 allowed = (offset >= -reach_left) & (offset <= reach_right)
                 masked.append(jnp.where(allowed, turned, -1e30))
         highest = functools.reduce(jnp.maximum, masked)
@@ -345,34 +356,28 @@
 
     backs = {}
 
-    def finish(pair):
-        blended = []
-        for i in pair:
-            scale = 1.0 / l_ref[i]
-            blended.append(
-                jnp.concatenate(
-                    [
-                        (acc_ref[i, pl.ds(HEAD_DIM * h, HEAD_DIM)] * scale[h : h + 1]).astype(BF16)
-                        for h in range(HEADS)
-                    ],
-                    axis=0,
-                )
-            )
-        mixed = product(wo_ref[...], jnp.concatenate(blended, axis=1))
-        for n, i in enumerate(pair):
-            done = (stream_ref[i].astype(F32) + mixed[:, LANES * n : LANES * (n + 1)]).astype(BF16)
-            done_ref[i] = done
-            backs[i] = remote(
-                done_ref.at[i], back_ref.at[mine], bs_sem.at[i], br_sem.at[mine], (F * team + i, ih)
-            )
-
-            @pl.when(mine != i)
-            def _():
-                backs[i].start()
-
-            @pl.when(mine == i)
-            def _():
-                back_ref[mine] = done
+    def finish(i):
+        scale = 1.0 / l_ref[i]
+        blended = jnp.concatenate(
+            [
+                (acc_ref[i, pl.ds(HEAD_DIM * h, HEAD_DIM)] * scale[h : h + 1]).astype(BF16)
+                for h in range(HEADS)
+            ],
+            axis=0,
+        )
+        done = (stream_ref[i].astype(F32) + product(wo_ref[...], blended)).astype(BF16)
+        done_ref[i] = done
+        backs[i] = remote(
+            done_ref.at[i], back_ref.at[mine], bs_sem.at[i], br_sem.at[mine], (F * team + i, ih)
+        )
+
+        @pl.when(mine != i)
+        def _():
+            backs[i].start()
+
+        @pl.when(mine == i)
+        def _():
+            back_ref[mine] = done
 
     loop(0, F, (2, 3, 4, 5), True)
 
@@ -381,22 +386,29 @@
         edge_arrived(3)
         halo_arrived(6)
         halo_arrived(7)
-        before = roll(silu(near_ref[5].astype(F32)), WIDE)
-        keys(6, temporal(6, 2, before, edge_frame(3, True, F - 1))[1])
-        loop(2, 4, (6, 7), False)
-
-    finish((2, 3))
 
     @pl.when(team > 0)
     def _():
         edge_arrived(0)
         halo_arrived(0)
         halo_arrived(1)
-        after = roll(silu(near_ref[2].astype(F32)), -WIDE)
-        keys(0, temporal(0, 2, edge_frame(0, True, 0), after)[1])
-        loop(0, 2, (0, 1), False)
-
-    finish((0, 1))
+
+    outside = (0, 1, 6, 7)
+    there = (team > 0, team > 0, team < teams - 1, team < teams - 1)
+    normed = temporal(
+        [jnp.where(there[n], near_ref[outside[n]].astype(F32), 0.0) for n in range(F)],
+        [edge_frame(0, team > 0, 0), None, rim_ref[1], None],
+        [None, rim_ref[0], None, edge_frame(3, team < teams - 1, F - 1)],
+    )[1]
+    made = product(wqkv_ref[pl.ds(C, 2 * C)], normed)
+    for n, m in enumerate(outside):
+        part = made[:, LANES * n : LANES * (n + 1)].astype(BF16)
+        k_ref[m] = part[:C]
+        for r in range(F):
+            v_ref[r, m] = roll(part[C:], -WIDE * r)
+    for i, blocks, known in ((2, (6, 7), there[2]), (3, (6, 7), there[2]), (0, (0, 1), there[0]), (1, (0, 1), there[0])):
+        attend(i, blocks, False, known)
+        finish(i)
 
     for step in (1, 3, 2):
         member = lax.rem(mine + step, F)
@@ -459,6 +471,7 @@
             pltpu.VMEM((F,) + frame, BF16),
             pltpu.VMEM((F,) + frame, BF16),
             pltpu.VMEM((F,) + frame, BF16),
+            pltpu.VMEM((2,) + frame, F32),
             pltpu.VMEM((F, F) + frame, BF16),
             pltpu.VMEM((2 * F,) + frame, BF16),
             pltpu.VMEM((F, 2 * F) + frame, BF16),
@@ -478,9 +491,24 @@
             pltpu.SemaphoreType.DMA((F,)),
         ],
         compiler_params=pltpu.CompilerParams(
-            collective_id=0, has_side_effects=True, vmem_limit_bytes=62 * 1024 * 1024
+            collective_id=0, has_side_effects=True, vmem_limit_bytes=40 * 1024 * 1024
         ),
-    )(win_left, win_right, frames_in, conv_spatial, conv_temporal, w_query, w_key, w_value, w_out)
+    )(
+        *(
+            pltpu.with_memory_space_constraint(v, pltpu.HBM)
+            for v in (
+                win_left,
+                win_right,
+                frames_in,
+                conv_spatial,
+                conv_temporal,
+                w_query,
+                w_key,
+                w_value,
+                w_out,
+            )
+        )
+    )
 
 
 def solution(mesh):

time: 41.6 us -> 37.4 us (0.90)
  the two profiles are of different devices: /device:TPU:2 before, /device:TPU:16 now
where the time goes in v4:
time: 37.4 us; the launch traced here: 37.2 us
  Pallas kernels  36.5 us (98%)
  local copies, waits for them, and re-layouts  0.73 us (2%)
    pallas_call x1, Pallas kernels, per_device(): pl.pallas_call(kernel, out_shape=jax.ShapeDtypeStruct(frames_in.shape, BF...  36.5 us

profile of v4, /device:TPU:16, one launch (start us, length us, event | category | flops | bytes accessed | tf_op | source)
XLA Modules:
  0.0 37.2 jit_solution(15146898070009550175)
XLA Ops:
  0.0 36.5 %shard_map.91 = bf16[4,320,128]{2,1,0:T(8,128)(2,1)S(1)} custom-call(s32[5]{0:T(128)} %wl_hbm.1, s32[5]{0:T(128)} %wr_hbm.1, bf16[4,320,128]{2,1,0:T(8,128)(2,1)} %x_hbm.1, bf16[320,2880]{1,0:T(8,128)(2,1)} %cs_hbm.1, bf16[320,960]{1,0:T(8,128)(2,1)} %ct_hbm.1, bf16[320,320]{1,0:T(8,128)(2,1)} %wq_hbm.1, bf16[320,320]{1,0:T(8,128)(2,1)} %wk_hbm.1, ...), custom_call_target="tpu_custom_call" | custom-call | tf_op jit(solution)/shard_map/pallas_call | solution.py:450
  36.5 0.7 %copy.11 = bf16[4,320,128]{2,1,0:T(8,128)(2,1)} copy(bf16[4,320,128]{2,1,0:T(8,128)(2,1)S(1)} %shard_map.91) | data formatting | bytes 655360

commit v5 on v4

--- a/solution.py
+++ b/solution.py
@@ -14,6 +14,7 @@
 F = 4
 LANES = 128
 QUARTER = C // F
+COLUMN = 16
 MESH = pl.DeviceIdType.MESH
 F32 = jnp.float32
 BF16 = jnp.bfloat16
@@ -75,6 +76,7 @@
     zr_sem,
     bs_sem,
     br_sem,
+    ok_sem,
 ):
     nt = lax.axis_size("tm")
     nh = lax.axis_size("height")
@@ -111,16 +113,10 @@
 
     @pl.when(team > 0)
     def _():
-        for dev in ((F * earlier + mine, ih), (F * earlier + 1, ih), (F * earlier + 3, ih)):
-            pl.semaphore_signal(barrier, inc=1, device_id=dev, device_id_type=MESH)
-
-    @pl.when(team < teams - 1)
-    def _():
-        for dev in ((F * later + mine, ih), (F * later, ih), (F * later + 2, ih)):
-            pl.semaphore_signal(barrier, inc=1, device_id=dev, device_id_type=MESH)
-
-    has_later, has_earlier = jnp.where(team < teams - 1, 1, 0), jnp.where(team > 0, 1, 0)
-    greetings = len(friends) + has_later * (1 + F * odd) + has_earlier * (1 + F * (1 - odd))
+        for j in range(F):
+            pl.semaphore_signal(barrier, inc=1, device_id=(F * earlier + j, ih), device_id_type=MESH)
+
+    greetings = len(friends) + F * jnp.where(team < teams - 1, 1, 0)
 
     def remote(src, dst, ssem, rsem, dev):
         return pltpu.make_async_remote_copy(
@@ -147,14 +143,27 @@
         fill(j + 1, silu(row))
 
     pl.semaphore_wait(barrier, greetings)
+    first = (team > 0) & (lax.rem(team, COLUMN) == 0)
     row_down = remote(
         taps_ref.at[F, pl.ds(C, C)], above_ref.at[0], hs_sem.at[0], hr_sem.at[0], (it, h_next)
     )
     row_up = remote(
         taps_ref.at[1, pl.ds(C, C)], above_ref.at[1], hs_sem.at[1], hr_sem.at[1], (it, h_prev)
     )
-    row_down.start()
-    row_up.start()
+
+    @pl.when(ih < nh - 1)
+    def _():
+        row_down.start()
+
+    @pl.when(ih > 0)
+    def _():
+        row_up.start()
+
+    @pl.when(team < teams - 1)
+    def _():
+        for j in range(F):
+            pl.semaphore_signal(ok_sem, inc=1, device_id=(F * later + j, ih), device_id_type=MESH)
+
 
     def around(j):
         return taps_ref[pl.ds(j, 3)].reshape(9 * C, LANES)
@@ -193,7 +202,7 @@
             edge_ref.at[j], far_ref.at[edge_slot], es_sem.at[j], er_sem.at[edge_slot], (F * edge_team + j, ih)
         )
 
-        @pl.when(edge_wanted)
+        @pl.when((odd == 1) & (team < teams - 1))
         def _():
             edges[j].start()
 
@@ -201,13 +210,32 @@
     inner = product(cs_ref[...], jnp.concatenate([around(1), around(2)], axis=1))
     settle(1, inner[:, :LANES])
     settle(2, inner[:, LANES:])
-    row_down.wait_recv()
-    row_up.wait_recv()
+
+    @pl.when(ih > 0)
+    def _():
+        row_down.wait_recv()
+
+    @pl.when(ih < nh - 1)
+    def _():
+        row_up.wait_recv()
+
     fill(0, jnp.where(ih > 0, above_ref[0].astype(F32), 0.0))
     fill(F + 1, jnp.where(ih < nh - 1, above_ref[1].astype(F32), 0.0))
     outer = product(cs_ref[...], jnp.concatenate([around(0), around(3)], axis=1))
     settle(0, outer[:, :LANES])
     settle(3, outer[:, LANES:])
+
+    def open_earlier():
+        pl.semaphore_wait(ok_sem, F)
+
+        @pl.when(odd == 0)
+        def _():
+            for j in range(F):
+                edges[j].start()
+
+    @pl.when((team > 0) & jnp.logical_not(first))
+    def _():
+        open_earlier()
 
     def swapped(member):
         return remote(
@@ -231,7 +259,7 @@
         )
         halos.append((late, copy))
 
-        @pl.when(wanted(late))
+        @pl.when(wanted(late) & (late | jnp.logical_not(first)))
         def _():
             copy.start()
 
@@ -243,6 +271,18 @@
         swapped(member).wait_recv()
         send_halo(member)
 
+    @pl.when(first)
+    def _():
+        open_earlier()
+        for m in (0, 1):
+            remote(
+                near_ref.at[2 + m],
+                near_ref.at[6 + m],
+                zs_sem.at[m],
+                zr_sem.at[6 + m],
+                (F * earlier + mine, ih),
+            ).start()
+
     def edge_arrived(slot):
         remote(edge_ref.at[0], far_ref.at[slot], es_sem.at[0], er_sem.at[slot], (it, h_next)).wait_recv()
 
@@ -262,27 +302,28 @@
         return jnp.concatenate([roll(block, WIDE * (place - n)) for n in range(F)], axis=0)
 
     def temporal(values, lefts, rights):
+        count = len(values)
         ahead, behind = [], []
-        for m in range(F):
+        for m in range(count):
             moving = silu(values[m])
             steps_ref[m, pl.ds(C, C)] = moving.astype(BF16)
             ahead.append(roll(moving, WIDE))
             behind.append(roll(moving, -WIDE))
-        for m in range(F):
+        for m in range(count):
             left = ahead[m - 1] if lefts[m] is None else lefts[m]
             right = behind[m + 1] if rights[m] is None else rights[m]
             steps_ref[m, pl.ds(0, C)] = jnp.where(group == 0, left, ahead[m]).astype(BF16)
             steps_ref[m, pl.ds(2 * C, C)] = jnp.where(group == F - 1, right, behind[m]).astype(BF16)
-        total = product(ct_ref[...], jnp.concatenate([steps_ref[m] for m in range(F)], axis=1))
+        total = product(ct_ref[...], jnp.concatenate([steps_ref[m] for m in range(count)], axis=1))
         streams, normed = [], []
-        for m in range(F):
+        for m in range(count):
             stream = (values[m] + total[:, LANES * m : LANES * (m + 1)]).astype(BF16)
             wide = stream.astype(F32)
             centred = wide - jnp.sum(wide, axis=0, keepdims=True) * (1.0 / C)
             spread = jnp.sum(centred * centred, axis=0, keepdims=True) * (1.0 / C)
             streams.append(stream)
             normed.append((centred * lax.rsqrt(spread + 1e-05)).astype(BF16))
-        return streams, jnp.concatenate(normed, axis=1), behind[0], ahead[F - 1]
+        return streams, jnp.concatenate(normed, axis=1), behind[0], ahead[count - 1]
 
     streams, normed, first_frame, last_frame = temporal(
         [near_ref[2 + i].astype(F32) for i in range(F)],
@@ -356,59 +397,72 @@
 
     backs = {}
 
-    def finish(i):
-        scale = 1.0 / l_ref[i]
-        blended = jnp.concatenate(
-            [
-                (acc_ref[i, pl.ds(HEAD_DIM * h, HEAD_DIM)] * scale[h : h + 1]).astype(BF16)
-                for h in range(HEADS)
-            ],
-            axis=0,
-        )
-        done = (stream_ref[i].astype(F32) + product(wo_ref[...], blended)).astype(BF16)
-        done_ref[i] = done
-        backs[i] = remote(
-            done_ref.at[i], back_ref.at[mine], bs_sem.at[i], br_sem.at[mine], (F * team + i, ih)
-        )
-
-        @pl.when(mine != i)
-        def _():
-            backs[i].start()
-
-        @pl.when(mine == i)
-        def _():
-            back_ref[mine] = done
+    def finish(pair):
+        blended = []
+        for i in pair:
+            scale = 1.0 / l_ref[i]
+            blended.append(
+                jnp.concatenate(
+                    [
+                        (acc_ref[i, pl.ds(HEAD_DIM * h, HEAD_DIM)] * scale[h : h + 1]).astype(BF16)
+                        for h in range(HEADS)
+                    ],
+                    axis=0,
+                )
+            )
+        mixed = product(wo_ref[...], jnp.concatenate(blended, axis=1))
+        for n, i in enumerate(pair):
+            done_ref[i] = (stream_ref[i].astype(F32) + mixed[:, LANES * n : LANES * (n + 1)]).astype(BF16)
+        for i in pair:
+            backs[i] = remote(
+                done_ref.at[i], back_ref.at[mine], bs_sem.at[i], br_sem.at[mine], (F * team + i, ih)
+            )
+
+            @pl.when(mine != i)
+            def _():
+                backs[i].start()
+
+            @pl.when(mine == i)
+            def _():
+                back_ref[mine] = done_ref[i]
 
     loop(0, F, (2, 3, 4, 5), True)
 
-    @pl.when(team < teams - 1)
-    def _():
-        edge_arrived(3)
-        halo_arrived(6)
-        halo_arrived(7)
-
-    @pl.when(team > 0)
-    def _():
-        edge_arrived(0)
-        halo_arrived(0)
-        halo_arrived(1)
-
-    outside = (0, 1, 6, 7)
-    there = (team > 0, team > 0, team < teams - 1, team < teams - 1)
-    normed = temporal(
-        [jnp.where(there[n], near_ref[outside[n]].astype(F32), 0.0) for n in range(F)],
-        [edge_frame(0, team > 0, 0), None, rim_ref[1], None],
-        [None, rim_ref[0], None, edge_frame(3, team < teams - 1, F - 1)],
-    )[1]
-    made = product(wqkv_ref[pl.ds(C, 2 * C)], normed)
-    for n, m in enumerate(outside):
-        part = made[:, LANES * n : LANES * (n + 1)].astype(BF16)
-        k_ref[m] = part[:C]
-        for r in range(F):
-            v_ref[r, m] = roll(part[C:], -WIDE * r)
-    for i, blocks, known in ((2, (6, 7), there[2]), (3, (6, 7), there[2]), (0, (0, 1), there[0]), (1, (0, 1), there[0])):
-        attend(i, blocks, False, known)
-        finish(i)
+    def side(places, edge, known, lefts, rights, pair):
+        @pl.when(known)
+        def _():
+            edge_arrived(edge)
+            for place in places:
+                halo_arrived(place)
+
+        values = [jnp.where(known, near_ref[place].astype(F32), 0.0) for place in places]
+        normed = temporal(values, lefts(), rights())[1]
+        made = product(wqkv_ref[pl.ds(C, 2 * C)], normed)
+        for n, place in enumerate(places):
+            part = made[:, LANES * n : LANES * (n + 1)].astype(BF16)
+            k_ref[place] = part[:C]
+            for r in range(F):
+                v_ref[r, place] = roll(part[C:], -WIDE * r)
+        for i in pair:
+            attend(i, places, False, known)
+        finish(pair)
+
+    side(
+        (6, 7),
+        3,
+        team < teams - 1,
+        lambda: [rim_ref[1], None],
+        lambda: [None, edge_frame(3, team < teams - 1, F - 1)],
+        (2, 3),
+    )
+    side(
+        (0, 1),
+        0,
+        team > 0,
+        lambda: [edge_frame(0, team > 0, 0), None],
+        lambda: [None, rim_ref[0]],
+        (0, 1),
+    )
 
     for step in (1, 3, 2):
         member = lax.rem(mine + step, F)
@@ -422,8 +476,14 @@
             whole = jnp.where(group == j, roll(lines[j], WIDE * (j - f)), whole)
         out_ref[f] = whole.astype(BF16)
 
-    row_down.wait_send()
-    row_up.wait_send()
+    @pl.when(ih < nh - 1)
+    def _():
+        row_down.wait_send()
+
+    @pl.when(ih > 0)
+    def _():
+        row_up.wait_send()
+
     for j in range(F):
 
         @pl.when(mine != j)
@@ -489,6 +549,7 @@
             pltpu.SemaphoreType.DMA((2 * F,)),
             pltpu.SemaphoreType.DMA((F,)),
             pltpu.SemaphoreType.DMA((F,)),
+            pltpu.SemaphoreType.REGULAR,
         ],
         compiler_params=pltpu.CompilerParams(
             collective_id=0, has_side_effects=True, vmem_limit_bytes=40 * 1024 * 1024

time: 37.4 us -> 33.6 us (0.90)
  the two profiles are of different devices: /device:TPU:16 before, /device:TPU:24 now
where the time goes in v5:
time: 33.6 us; the launch traced here: 33.5 us
  Pallas kernels  32.7 us (97%)
  local copies, waits for them, and re-layouts  0.73 us (2%)
    pallas_call x1, Pallas kernels, per_device(): pl.pallas_call(kernel, out_shape=jax.ShapeDtypeStruct(frames_in.shape, BF...  32.7 us
    unnamed x1, local copies, waits for them, and re-layouts  0.73 us

profile of v5, /device:TPU:24, one launch (start us, length us, event | category | flops | bytes accessed | tf_op | source)
XLA Modules:
  0.0 33.5 jit_solution(8097698639965195943)
XLA Ops:
  0.0 32.7 %shard_map.91 = bf16[4,320,128]{2,1,0:T(8,128)(2,1)S(1)} custom-call(s32[5]{0:T(128)} %wl_hbm.1, s32[5]{0:T(128)} %wr_hbm.1, bf16[4,320,128]{2,1,0:T(8,128)(2,1)} %x_hbm.1, bf16[320,2880]{1,0:T(8,128)(2,1)} %cs_hbm.1, bf16[320,960]{1,0:T(8,128)(2,1)} %ct_hbm.1, bf16[320,320]{1,0:T(8,128)(2,1)} %wq_hbm.1, bf16[320,320]{1,0:T(8,128)(2,1)} %wk_hbm.1, ...), custom_call_target="tpu_custom_call" | custom-call | tf_op jit(solution)/shard_map/pallas_call | solution.py:510
  32.7 0.7 %copy.11 = bf16[4,320,128]{2,1,0:T(8,128)(2,1)} copy(bf16[4,320,128]{2,1,0:T(8,128)(2,1)S(1)} %shard_map.91) | data formatting | bytes 655360

commit v6 on v5

--- a/solution.py
+++ b/solution.py
@@ -76,6 +76,7 @@
     zr_sem,
     bs_sem,
     br_sem,
+    ds_sem,
     ok_sem,
 ):
     nt = lax.axis_size("tm")
@@ -144,6 +145,9 @@
 
     pl.semaphore_wait(barrier, greetings)
     first = (team > 0) & (lax.rem(team, COLUMN) == 0)
+    direct = (team < teams - 1) & (lax.rem(team, COLUMN) == COLUMN - 1)
+    outer_row = jnp.where(mine == 0, 1, jnp.where(mine == F - 1, 1, 0))
+    straight = {}
     row_down = remote(
         taps_ref.at[F, pl.ds(C, C)], above_ref.at[0], hs_sem.at[0], hr_sem.at[0], (it, h_next)
     )
@@ -180,18 +184,6 @@
         settled = (rows_ref[j] + spatial).astype(BF16)
         settled_ref[j] = settled
         wide = settled.astype(F32)
-        swaps[j] = remote(
-            settled_ref.at[j], near_ref.at[2 + mine], gs_sem.at[j], gr_sem.at[mine], (F * team + j, ih)
-        )
-
-        @pl.when(mine != j)
-        def _():
-            swaps[j].start()
-
-        @pl.when(mine == j)
-        def _():
-            near_ref[2 + j] = settled
-
         block = jnp.zeros((QUARTER, LANES), F32)
         for n in range(F):
             part = wide[QUARTER * n : QUARTER * (n + 1)]
@@ -206,10 +198,36 @@
         def _():
             edges[j].start()
 
+        swaps[j] = remote(
+            settled_ref.at[j], near_ref.at[2 + mine], gs_sem.at[j], gr_sem.at[mine], (F * team + j, ih)
+        )
+
+        if j in (0, F - 1):
+            place = jnp.maximum(mine - 2, 0)
+            straight[j] = remote(
+                settled_ref.at[j], near_ref.at[place], ds_sem.at[j], zr_sem.at[place], (F * later + j, ih)
+            )
+
+            @pl.when(direct & (mine >= 2))
+            def _():
+                straight[j].start()
+
+        @pl.when(mine != j)
+        def _():
+            swaps[j].start()
+
+        @pl.when(mine == j)
+        def _():
+            near_ref[2 + j] = settled
+
     loads[1].wait()
     inner = product(cs_ref[...], jnp.concatenate([around(1), around(2)], axis=1))
     settle(1, inner[:, :LANES])
     settle(2, inner[:, LANES:])
+    middle = product(
+        cs_ref[:, 1024:1920],
+        jnp.concatenate([taps_ref[1, pl.ds(64, 896)], taps_ref[F, pl.ds(64, 896)]], axis=1),
+    )
 
     @pl.when(ih > 0)
     def _():
@@ -221,7 +239,13 @@
 
     fill(0, jnp.where(ih > 0, above_ref[0].astype(F32), 0.0))
     fill(F + 1, jnp.where(ih < nh - 1, above_ref[1].astype(F32), 0.0))
-    outer = product(cs_ref[...], jnp.concatenate([around(0), around(3)], axis=1))
+    outer = product(
+        cs_ref[:, 0:1024], jnp.concatenate([around(0)[0:1024], around(3)[0:1024]], axis=1)
+    )
+    outer += product(
+        cs_ref[:, 1920:2880], jnp.concatenate([taps_ref[2], taps_ref[F + 1]], axis=1)
+    )
+    outer += middle
     settle(0, outer[:, :LANES])
     settle(3, outer[:, LANES:])
 
@@ -257,9 +281,10 @@
             zr_sem.at[place],
             (F * jnp.where(late, later, earlier) + mine, ih),
         )
-        halos.append((late, copy))
-
-        @pl.when(wanted(late) & (late | jnp.logical_not(first)))
+        sent = wanted(late) & jnp.logical_not(late & direct & (outer_row == 1))
+        halos.append((sent, copy))
+
+        @pl.when(sent & (late | jnp.logical_not(first)))
         def _():
             copy.start()
 
@@ -271,31 +296,11 @@
         swapped(member).wait_recv()
         send_halo(member)
 
-    @pl.when(first)
-    def _():
-        open_earlier()
-        for m in (0, 1):
-            remote(
-                near_ref.at[2 + m],
-                near_ref.at[6 + m],
-                zs_sem.at[m],
-                zr_sem.at[6 + m],
-                (F * earlier + mine, ih),
-            ).start()
-
     def edge_arrived(slot):
         remote(edge_ref.at[0], far_ref.at[slot], es_sem.at[0], er_sem.at[slot], (it, h_next)).wait_recv()
 
     def halo_arrived(place):
         remote(near_ref.at[2], near_ref.at[place], zs_sem.at[0], zr_sem.at[place], (it, h_next)).wait_recv()
-
-    @pl.when(team > 0)
-    def _():
-        edge_arrived(1)
-
-    @pl.when(team < teams - 1)
-    def _():
-        edge_arrived(2)
 
     def edge_frame(slot, there, place):
         block = silu(jnp.where(there, far_ref[slot].astype(F32), 0.0))
@@ -323,24 +328,27 @@
             spread = jnp.sum(centred * centred, axis=0, keepdims=True) * (1.0 / C)
             streams.append(stream)
             normed.append((centred * lax.rsqrt(spread + 1e-05)).astype(BF16))
-        return streams, jnp.concatenate(normed, axis=1), behind[0], ahead[count - 1]
-
-    streams, normed, first_frame, last_frame = temporal(
-        [near_ref[2 + i].astype(F32) for i in range(F)],
-        [edge_frame(1, team > 0, 0), None, None, None],
-        [None, None, None, edge_frame(2, team < teams - 1, F - 1)],
-    )
-    rim_ref[0] = first_frame
-    rim_ref[1] = last_frame
-    made = product(wqkv_ref[...], normed)
-    for i in range(F):
-        stream_ref[i] = streams[i]
-        part = made[:, LANES * i : LANES * (i + 1)]
-        query, value = part[:C].astype(BF16), part[2 * C :].astype(BF16)
-        for r in range(F):
-            q_ref[r, i] = roll(query, WIDE * r)
-            v_ref[r, 2 + i] = roll(value, -WIDE * r)
-        k_ref[2 + i] = part[C : 2 * C].astype(BF16)
+        return streams, jnp.concatenate(normed, axis=1), behind[0]
+
+    def side_keys(places, edge, lefts, rights):
+        edge_arrived(edge)
+        for place in places:
+            halo_arrived(place)
+        normed = temporal([near_ref[place].astype(F32) for place in places], lefts(), rights())[1]
+        made = product(wqkv_ref[pl.ds(C, 2 * C)], normed)
+        for n, place in enumerate(places):
+            part = made[:, LANES * n : LANES * (n + 1)].astype(BF16)
+            k_ref[place] = part[:C]
+            for r in range(F):
+                v_ref[r, place] = roll(part[C:], -WIDE * r)
+
+    def next_keys():
+        side_keys(
+            (6, 7),
+            3,
+            lambda: [roll(silu(near_ref[5].astype(F32)), WIDE), None],
+            lambda: [None, edge_frame(3, True, F - 1)],
+        )
 
     head_row = lax.broadcasted_iota(jnp.int32, (8, LANES), 0)
     lane_frame = lax.shift_right_logical(lax.broadcasted_iota(jnp.int32, (8, LANES), 1), 5)
@@ -356,7 +364,7 @@
         0.0,
     ).astype(BF16)
 
-    def attend(i, blocks, fresh, known=None):
+    def attend(i, blocks, fresh):
         masked = []
         for m in blocks:
             products = jnp.concatenate([q_ref[r, i] * k_ref[m] for r in range(F)], axis=1)
@@ -364,8 +372,6 @@
             for r in range(F):
                 turned = roll(scores[:, LANES * r : LANES * (r + 1)], -WIDE * r)
                 offset = F * (m - 2 - i) + jnp.bitwise_and(lane_frame + r, F - 1) - lane_frame
-                if known is not None:
-                    offset = jnp.where(known, offset, 2 * LANES)
                 allowed = (offset >= -reach_left) & (offset <= reach_right)
                 masked.append(jnp.where(allowed, turned, -1e30))
         highest = functools.reduce(jnp.maximum, masked)
@@ -395,7 +401,10 @@
 
         lax.fori_loop(low, high, step, 0)
 
-    backs = {}
+    backs = [
+        remote(done_ref.at[i], back_ref.at[mine], bs_sem.at[i], br_sem.at[mine], (F * team + i, ih))
+        for i in range(F)
+    ]
 
     def finish(pair):
         blended = []
@@ -414,9 +423,6 @@
         for n, i in enumerate(pair):
             done_ref[i] = (stream_ref[i].astype(F32) + mixed[:, LANES * n : LANES * (n + 1)]).astype(BF16)
         for i in pair:
-            backs[i] = remote(
-                done_ref.at[i], back_ref.at[mine], bs_sem.at[i], br_sem.at[mine], (F * team + i, ih)
-            )
 
             @pl.when(mine != i)
             def _():
@@ -426,48 +432,112 @@
             def _():
                 back_ref[mine] = done_ref[i]
 
-    loop(0, F, (2, 3, 4, 5), True)
-
-    def side(places, edge, known, lefts, rights, pair):
-        @pl.when(known)
-        def _():
-            edge_arrived(edge)
-            for place in places:
-                halo_arrived(place)
-
-        values = [jnp.where(known, near_ref[place].astype(F32), 0.0) for place in places]
-        normed = temporal(values, lefts(), rights())[1]
-        made = product(wqkv_ref[pl.ds(C, 2 * C)], normed)
-        for n, place in enumerate(places):
-            part = made[:, LANES * n : LANES * (n + 1)].astype(BF16)
-            k_ref[place] = part[:C]
+    def own_keys(members):
+        low, high = members[0], members[-1]
+        if low == 0:
+            left = edge_frame(1, team > 0, 0)
+        else:
+            left = roll(silu(near_ref[1 + low].astype(F32)), WIDE)
+        if high == F - 1:
+            right = edge_frame(2, team < teams - 1, F - 1)
+        else:
+            right = roll(silu(near_ref[3 + high].astype(F32)), -WIDE)
+        count = len(members)
+        streams, normed, first_frame = temporal(
+            [near_ref[2 + i].astype(F32) for i in members],
+            [left] + [None] * (count - 1),
+            [None] * (count - 1) + [right],
+        )
+        if low == 0:
+            rim_ref[...] = first_frame
+        made = product(wqkv_ref[...], normed)
+        for n, i in enumerate(members):
+            stream_ref[i] = streams[n]
+            part = made[:, LANES * n : LANES * (n + 1)]
+            query, value = part[:C].astype(BF16), part[2 * C :].astype(BF16)
             for r in range(F):
-                v_ref[r, place] = roll(part[C:], -WIDE * r)
+                q_ref[r, i] = roll(query, WIDE * r)
+                v_ref[r, 2 + i] = roll(value, -WIDE * r)
+            k_ref[2 + i] = part[C : 2 * C].astype(BF16)
+
+    @pl.when(team < teams - 1)
+    def _():
+        edge_arrived(2)
+
+    @pl.when(jnp.logical_not(first))
+    def _():
+        @pl.when(team > 0)
+        def _():
+            edge_arrived(1)
+
+        own_keys((0, 1, 2, 3))
+        loop(0, F, (2, 3, 4, 5), True)
+
+    @pl.when(first)
+    def _():
+        own_keys((1, 2, 3))
+        open_earlier()
+        for m in (0, 1):
+            remote(
+                near_ref.at[2 + m],
+                near_ref.at[6 + m],
+                zs_sem.at[m],
+                zr_sem.at[6 + m],
+                (F * earlier + mine, ih),
+            ).start()
+
+        loop(1, F, (3, 4, 5), True)
+
+        @pl.when(team < teams - 1)
+        def _():
+            next_keys()
+
+        edge_arrived(1)
+        own_keys((0,))
+        attend(0, (2, 3, 4), True)
+        attend(1, (2,), False)
+        attend(2, (2,), False)
+
+
+    def side(places, pair):
         for i in pair:
-            attend(i, places, False, known)
+            attend(i, places, False)
         finish(pair)
 
-    side(
-        (6, 7),
-        3,
-        team < teams - 1,
-        lambda: [rim_ref[1], None],
-        lambda: [None, edge_frame(3, team < teams - 1, F - 1)],
-        (2, 3),
-    )
-    side(
-        (0, 1),
-        0,
-        team > 0,
-        lambda: [edge_frame(0, team > 0, 0), None],
-        lambda: [None, rim_ref[0]],
-        (0, 1),
-    )
+    @pl.when(team == 0)
+    def _():
+        finish((0, 1))
+
+    @pl.when((team < teams - 1) & jnp.logical_not(first))
+    def _():
+        next_keys()
+
+    @pl.when(team < teams - 1)
+    def _():
+        side((6, 7), (2, 3))
+
+    @pl.when(team == teams - 1)
+    def _():
+        finish((2, 3))
+
+    @pl.when(team > 0)
+    def _():
+        side_keys(
+            (0, 1),
+            0,
+            lambda: [edge_frame(0, True, 0), None],
+            lambda: [None, rim_ref[...]],
+        )
+        side((0, 1), (0, 1))
 
     for step in (1, 3, 2):
         member = lax.rem(mine + step, F)
         remote(
-            done_ref.at[0], back_ref.at[member], bs_sem.at[0], br_sem.at[member], (it, h_next)
+            done_ref.at[0],
+            back_ref.at[member],
+            bs_sem.at[0],
+            br_sem.at[member],
+            (it, h_next),
         ).wait_recv()
     lines = [back_ref[j].astype(F32) for j in range(F)]
     for f in range(F):
@@ -489,15 +559,24 @@
         @pl.when(mine != j)
         def _():
             swaps[j].wait_send()
+
+        @pl.when(mine != j)
+        def _():
             backs[j].wait_send()
 
         @pl.when(edge_wanted)
         def _():
             edges[j].wait_send()
 
-    for late, copy in halos:
-
-        @pl.when(wanted(late))
+    for j in (0, F - 1):
+
+        @pl.when(direct & (mine >= 2))
+        def _():
+            straight[j].wait_send()
+
+    for sent, copy in halos:
+
+        @pl.when(sent)
         def _():
             copy.wait_send()
 
@@ -531,7 +610,7 @@
             pltpu.VMEM((F,) + frame, BF16),
             pltpu.VMEM((F,) + frame, BF16),
             pltpu.VMEM((F,) + frame, BF16),
-            pltpu.VMEM((2,) + frame, F32),
+            pltpu.VMEM(frame, F32),
             pltpu.VMEM((F, F) + frame, BF16),
             pltpu.VMEM((2 * F,) + frame, BF16),
             pltpu.VMEM((F, 2 * F) + frame, BF16),
@@ -547,6 +626,7 @@
             pltpu.SemaphoreType.DMA((F,)),
             pltpu.SemaphoreType.DMA((F,)),
             pltpu.SemaphoreType.DMA((2 * F,)),
+            pltpu.SemaphoreType.DMA((F,)),
             pltpu.SemaphoreType.DMA((F,)),
             pltpu.SemaphoreType.DMA((F,)),
             pltpu.SemaphoreType.REGULAR,

time: 33.6 us -> 32.7 us (0.973)
  Pallas kernels: 32.7 us -> 31.9 us
    pallas_call x1, Pallas kernels: 32.7 us -> 31.9 us  [per_device(): pl.pallas_call(kernel, out_shape=jax.ShapeDtypeStruct(frames_in.shape, BF...]
where the time goes in v6:
time: 32.7 us; the launch traced here: 32.6 us
  Pallas kernels  31.9 us (98%)
  local copies, waits for them, and re-layouts  0.73 us (2%)
    pallas_call x1, Pallas kernels, per_device(): pl.pallas_call(kernel, out_shape=jax.ShapeDtypeStruct(frames_in.shape, BF...  31.9 us
    unnamed x1, local copies, waits for them, and re-layouts  0.73 us

profile of v6, /device:TPU:24, one launch (start us, length us, event | category | flops | bytes accessed | tf_op | source)
XLA Modules:
  0.0 32.6 jit_solution(11790340602931874742)
XLA Ops:
  0.0 31.9 %shard_map.91 = bf16[4,320,128]{2,1,0:T(8,128)(2,1)S(1)} custom-call(s32[5]{0:T(128)} %wl_hbm.1, s32[5]{0:T(128)} %wr_hbm.1, bf16[4,320,128]{2,1,0:T(8,128)(2,1)} %x_hbm.1, bf16[320,2880]{1,0:T(8,128)(2,1)} %cs_hbm.1, bf16[320,960]{1,0:T(8,128)(2,1)} %ct_hbm.1, bf16[320,320]{1,0:T(8,128)(2,1)} %wq_hbm.1, bf16[320,320]{1,0:T(8,128)(2,1)} %wk_hbm.1, ...), custom_call_target="tpu_custom_call" | custom-call | tf_op jit(solution)/shard_map/pallas_call | solution.py:589
  31.9 0.7 %copy.11 = bf16[4,320,128]{2,1,0:T(8,128)(2,1)} copy(bf16[4,320,128]{2,1,0:T(8,128)(2,1)S(1)} %shard_map.91) | data formatting | bytes 655360

commit v7 on v6

--- a/solution.py
+++ b/solution.py
@@ -146,7 +146,7 @@
     pl.semaphore_wait(barrier, greetings)
     first = (team > 0) & (lax.rem(team, COLUMN) == 0)
     direct = (team < teams - 1) & (lax.rem(team, COLUMN) == COLUMN - 1)
-    outer_row = jnp.where(mine == 0, 1, jnp.where(mine == F - 1, 1, 0))
+    outer_row = jnp.where(mine == 0, 1, 0)
     straight = {}
     row_down = remote(
         taps_ref.at[F, pl.ds(C, C)], above_ref.at[0], hs_sem.at[0], hr_sem.at[0], (it, h_next)
@@ -202,7 +202,7 @@
             settled_ref.at[j], near_ref.at[2 + mine], gs_sem.at[j], gr_sem.at[mine], (F * team + j, ih)
         )
 
-        if j in (0, F - 1):
+        if j == 0:
             place = jnp.maximum(mine - 2, 0)
             straight[j] = remote(
                 settled_ref.at[j], near_ref.at[place], ds_sem.at[j], zr_sem.at[place], (F * later + j, ih)
@@ -568,7 +568,7 @@
         def _():
             edges[j].wait_send()
 
-    for j in (0, F - 1):
+    for j in (0,):
 
         @pl.when(direct & (mine >= 2))
         def _():

time: 32.7 us -> 32.6 us (level)
  no operation moved by 1% of the time
where the time goes in v7:
time: 32.6 us; the launch traced here: 32.4 us
  Pallas kernels  31.7 us (97%)
  local copies, waits for them, and re-layouts  0.73 us (2%)
    pallas_call x1, Pallas kernels, per_device(): pl.pallas_call(kernel, out_shape=jax.ShapeDtypeStruct(frames_in.shape, BF...  31.7 us
    unnamed x1, local copies, waits for them, and re-layouts  0.73 us

profile of v7, /device:TPU:24, one launch (start us, length us, event | category | flops | bytes accessed | tf_op | source)
XLA Modules:
  0.0 32.4 jit_solution(2099669001590484820)
XLA Ops:
  0.0 31.7 %shard_map.91 = bf16[4,320,128]{2,1,0:T(8,128)(2,1)S(1)} custom-call(s32[5]{0:T(128)} %wl_hbm.1, s32[5]{0:T(128)} %wr_hbm.1, bf16[4,320,128]{2,1,0:T(8,128)(2,1)} %x_hbm.1, bf16[320,2880]{1,0:T(8,128)(2,1)} %cs_hbm.1, bf16[320,960]{1,0:T(8,128)(2,1)} %ct_hbm.1, bf16[320,320]{1,0:T(8,128)(2,1)} %wq_hbm.1, bf16[320,320]{1,0:T(8,128)(2,1)} %wk_hbm.1, ...), custom_call_target="tpu_custom_call" | custom-call | tf_op jit(solution)/shard_map/pallas_call | solution.py:589
  31.7 0.7 %copy.11 = bf16[4,320,128]{2,1,0:T(8,128)(2,1)} copy(bf16[4,320,128]{2,1,0:T(8,128)(2,1)S(1)} %shard_map.91) | data formatting | bytes 655360
